TPU v7x, 256 devices: a whole 4x4x8 slice. The times are simulated.
256 devices in a mesh: side: 2 (over core), shard: 16 (over y, z_lo), tp: 8 (over z_hi, x).
Axes of the slice: x: 4, y: 4, z: 8 (z_hi: 2, z_lo: 4; z = z_hi * 4 + z_lo), core: 2. Of those that a mesh axis runs over, the one named last changes fastest.
Arguments:
- tokens: bfloat16 [32, 4096], P(None, 'shard'), may hold values from -24 to 24
- lengths: int32 [32], replicated, may hold values from 1 to 4096, as said below
- kv_cache: bfloat16 [2, 32, 4096, 8, 256], P('side', 'shard', None, 'tp'), may hold values from -104 to 104
- attn_gain: float32 [2, 4096], P('side', 'shard'), may hold values from 0.1 to 1.9
- qkv_weight: bfloat16 [2, 4096, 8, 768], P('side', 'shard', 'tp'), may hold values from -0.09375 to 0.09375
- out_weight: bfloat16 [2, 8, 512, 4096], P('side', 'tp', None, 'shard'), may hold values from -0.25 to 0.25
- ffn_gain: float32 [2, 4096], P('side', 'shard'), may hold values from 0.1 to 1.9
- gate_up: bfloat16 [2, 4096, 2, 14336], P('side', 'shard', None, 'tp'), may hold values from -0.09375 to 0.09375
- down_weight: bfloat16 [2, 14336, 4096], P('side', 'tp', 'shard'), may hold values from -0.046875 to 0.046875
Outputs:
- streams: bfloat16 [2, 32, 4096], P('side', None, 'shard')
- row_scales: float32 [2, 2, 32], P('side')
Inputs may be any that keep to these rules, and one draw needn't show every extreme that they name: `lengths`: some sequence has exactly 4096 cached positions.
All inputs are finite; a program needn't handle non-finite values.
Results may differ from a plain program's by a relative error of at most 0.03.
Values may be sent and summed in bfloat16 or wider, within the bound.
A program may use at most 64 MiB of HBM per device.

v0:
```python
import jax
import jax.numpy as jnp
from jax import lax
from jax.sharding import PartitionSpec as P

D = 4096
HD = 128
GROUP = 4


EPSILON = 1e-05
ROPE_BASE = 500000.0


def passed_along(shard, axis, by):
    size = lax.axis_size(axis)
    return lax.ppermute(shard, axis, [(i, (i + by) % size) for i in range(size)])


def rotate(vectors, positions):
    half_dim = vectors.shape[-1] // 2
    freqs = ROPE_BASE ** (-jnp.arange(half_dim, dtype=jnp.float32) * 2.0 / vectors.shape[-1])
    angles = positions.astype(jnp.float32)[:, None] * freqs[None, :]
    shape_out = (angles.shape[0],) + (1,) * (vectors.ndim - 2) + (half_dim,)
    cosine = jnp.cos(angles).reshape(shape_out)
    sine = jnp.sin(angles).reshape(shape_out)
    lower = vectors[..., :half_dim]
    upper = vectors[..., half_dim:]
    return jnp.concatenate([lower * cosine - upper * sine, upper * cosine + lower * sine], axis=-1)


def attend(incoming, own_lengths, own_cache, gain_row, qkv_part, out_part):
    own_count = own_cache.shape[0]
    kv_local = qkv_part.shape[1]
    values_f32 = incoming.astype(jnp.float32)
    square_sum = lax.psum(jnp.sum(values_f32 * values_f32, axis=1), "shard")
    factor = lax.rsqrt(square_sum / D + EPSILON)
    normed = (values_f32 * factor[:, None] * gain_row).astype(jnp.bfloat16)
    mixed = lax.psum_scatter(
        jnp.einsum("rd,dkc->rkc", normed, qkv_part, preferred_element_type=jnp.float32),
        "shard",
        scatter_dimension=0,
        tiled=True,
    )
    mixed = mixed.reshape(own_count, kv_local, GROUP + 2, HD)
    queries = rotate(mixed[:, :, :GROUP], own_lengths).astype(jnp.bfloat16)
    new_keys = rotate(mixed[:, :, GROUP], own_lengths).astype(jnp.bfloat16)
    new_values = mixed[:, :, GROUP + 1].astype(jnp.bfloat16)
    span_local = own_cache.shape[1]
    scores = jnp.einsum(
        "rkgh,rtkh->rkgt", queries, own_cache[..., :HD], preferred_element_type=jnp.float32
    ) * HD ** (-0.5)
    valid_mask = jnp.arange(span_local)[None, None, None, :] < own_lengths[:, None, None, None]
    own_score = jnp.sum(
        queries.astype(jnp.float32) * new_keys.astype(jnp.float32)[:, :, None, :], axis=-1
    ) * HD ** (-0.5)
    row_top = jnp.maximum(jnp.max(jnp.where(valid_mask, scores, -1e30), axis=-1), own_score)
    weights = jnp.where(valid_mask, jnp.exp(scores - row_top[..., None]), 0.0)
    own_weight = jnp.exp(own_score - row_top)
    row_total = jnp.sum(weights, axis=-1) + own_weight
    own_rounded = lax.optimization_barrier(own_weight.astype(jnp.bfloat16)).astype(jnp.float32)
    numerator = jnp.einsum(
        "rkgt,rtkh->rkgh",
        weights.astype(jnp.bfloat16),
        own_cache[..., HD:],
        preferred_element_type=jnp.float32,
    )
    numerator = numerator + own_rounded[..., None] * new_values.astype(jnp.float32)[:, :, None, :]
    attended = (
        (numerator / row_total[..., None])
        .astype(jnp.bfloat16)
        .reshape(own_count, kv_local, GROUP * HD)
    )
    projected = jnp.einsum(
        "rkc,kcd->rd",
        lax.all_gather(attended, "shard", axis=0, tiled=True),
        out_part,
        preferred_element_type=jnp.float32,
    )
    projected = lax.psum(projected, "tp")
    return ((values_f32 + projected).astype(jnp.bfloat16), factor)


def feed_forward(received, gain_row, gate_part, down_part):
    values_f32 = received.astype(jnp.float32)
    square_sum = lax.psum(jnp.sum(values_f32 * values_f32, axis=1), "shard")
    factor = lax.rsqrt(square_sum / D + EPSILON)
    normed = (values_f32 * factor[:, None] * gain_row).astype(jnp.bfloat16)
    both_terms = jnp.einsum("rd,dcf->rcf", normed, gate_part, preferred_element_type=jnp.float32)
    both_terms = lax.psum(both_terms, "shard")
    hidden_rows = (jax.nn.silu(both_terms[:, 0]) * both_terms[:, 1]).astype(jnp.bfloat16)
    partial_out = jnp.dot(hidden_rows, down_part, preferred_element_type=jnp.float32)
    summed = lax.psum(partial_out, "tp")
    return ((values_f32 + summed).astype(jnp.bfloat16), factor)


def reorder_rows(stacked, batch_count, shard_count, per_batch):
    shaped = stacked.reshape(batch_count, shard_count, per_batch)
    return jnp.transpose(shaped, (1, 0, 2)).reshape(shard_count * batch_count * per_batch)


def body(
    tokens, lengths, kv_cache, attn_gain, qkv_weight, out_weight, ffn_gain, gate_up, down_weight
):
    first_side = lax.axis_index("side") == 0
    shard_position = lax.axis_index("shard")
    shard_count = lax.axis_size("shard")
    batch_count = 1
    local_seqs = kv_cache.shape[1]
    per_batch = local_seqs // batch_count
    width_local = tokens.shape[1]
    token_grid = tokens.reshape(shard_count, batch_count, per_batch, width_local)
    length_grid = lengths.reshape(shard_count, batch_count, per_batch)
    cache = kv_cache[0]
    finished_first = []
    finished_second = []
    attn_factors = []
    ffn_factors = []
    previous = None
    for round_number in range(batch_count + 1):
        first_batch = min(round_number, batch_count - 1)
        second_batch = max(round_number - 1, 0)
        batch_index = jnp.where(first_side, first_batch, second_batch).astype(jnp.int32)
        fresh_rows = token_grid[:, first_batch].reshape(shard_count * per_batch, width_local)
        if previous is None:
            incoming = fresh_rows
        else:
            incoming = jnp.where(first_side, fresh_rows, previous)
        own_lengths = lax.dynamic_slice(
            length_grid, (shard_position, batch_index, jnp.int32(0)), (1, 1, per_batch)
        ).reshape(per_batch)
        attended, attn_factor = attend(
            incoming, own_lengths, cache, attn_gain[0], qkv_weight[0], out_weight[0]
        )
        received = passed_along(attended, "side", 1)
        previous, ffn_factor = feed_forward(received, ffn_gain[0], gate_up[0], down_weight[0])
        attn_factors.append(attn_factor)
        ffn_factors.append(ffn_factor)
        if round_number >= 1:
            finished_first.append(previous)
        if round_number < batch_count:
            finished_second.append(previous)
    first_rows = jnp.stack(finished_first).reshape(batch_count, shard_count, per_batch, width_local)
    second_rows = jnp.stack(finished_second).reshape(
        batch_count, shard_count, per_batch, width_local
    )
    result = jnp.where(first_side, first_rows, second_rows)
    result = jnp.transpose(result, (1, 0, 2, 3)).reshape(shard_count * local_seqs, width_local)
    attn_early = reorder_rows(
        jnp.stack(attn_factors[:batch_count]), batch_count, shard_count, per_batch
    )
    attn_late = reorder_rows(jnp.stack(attn_factors[1:]), batch_count, shard_count, per_batch)
    ffn_early = reorder_rows(
        jnp.stack(ffn_factors[:batch_count]), batch_count, shard_count, per_batch
    )
    ffn_late = reorder_rows(jnp.stack(ffn_factors[1:]), batch_count, shard_count, per_batch)
    attn_scale = jnp.where(first_side, attn_early, attn_late)
    ffn_scale = jnp.where(first_side, ffn_late, ffn_early)
    scales = jnp.stack([attn_scale, ffn_scale])
    return (result[None], scales[None])


def solution(mesh):
    in_specs = (
        P(None, "shard"),
        P(),
        P("side", "shard", None, "tp", None),
        P("side", "shard"),
        P("side", "shard", "tp", None),
        P("side", "tp", None, "shard"),
        P("side", "shard"),
        P("side", "shard", None, "tp"),
        P("side", "tp", "shard"),
    )
    out_specs = (P("side", None, "shard"), P("side", None, None))
    return jax.shard_map(body, mesh=mesh, in_specs=in_specs, out_specs=out_specs, check_vma=False)
```

profile of v0, /device:TPU:6, one launch (start us, length us, event | category | flops | bytes accessed | tf_op | source)
XLA Modules:
  0.0 1082.6 jit_solution(7546422157592179145)
XLA Ops:
  7.2 0.0 copy-start
  7.2 0.0 all-reduce.11.cloned.1.call-start
  7.2 1.0 fusion.40
  8.2 45.0 %psum.70 = f32[32]{0:T(128)S(1)} all-reduce(f32[32]{0:T(128)S(1)} %fusion.40), channel_id=1, replica_groups=mesh['side'=2,'shard'=16,'tp'=8] {'shard'}, use_global_device_ids=true, to_apply=%region_1.2 | all-reduce | flops 32 | bytes 256 | tf_op jit(solution)/shard_map/psum | solution.py:36
  53.2 1.9 convolution_bitcast_fusion.1
  55.1 0.0 all-reduce.11.cloned.1.call-update
  55.2 0.0 all-reduce.7.cloned.1.call-start
  55.2 0.7 reshape.564
  56.0 0.1 iota_compare_fusion
  56.1 0.1 multiply_cosine_fusion.1
  56.2 1.3 dynamic-slice
  58.1 147.0 %all-reduce.11.cloned.1.call-done = f32[32,1,768]{2,0,1:T(8,128)} async-done(((f32[32,1,768]{2,0,1:T(8,128)}), f32[32,1,768]{2,0,1:T(8,128)}) %all-reduce.11.cloned.1.call-update) | async-done | bytes 98320
  205.1 0.7 constant_dynamic-slice_fusion.1
  205.8 0.1 fusion.106
  206.0 0.1 maximum_convert_fusion
  206.0 0.1 subtract_convert_fusion.1
  206.1 0.2 multiply_reduce_fusion.1
  206.3 2.4 select_reduce_fusion.1
  208.7 0.2 fusion.28
  209.0 2.0 fusion.11
  211.0 40.0 %all_gather.6 = bf16[32,1,512]{2,1,0:T(2,128)(2,1)S(1)} all-gather(bf16[2,1,512]{2,1,0:T(2,128)(2,1)S(1)} %reshape.581), channel_id=1, replica_groups=mesh['side'=2,'shard'=16,'tp'=8] {'shard'}, dimensions={0}, use_global_device_ids=true | all-gather | bytes 34816 | tf_op jit(solution)/shard_map/all_gather | solution.py:76
  251.0 0.1 fusion.20
  251.2 45.9 %psum.71 = f32[32,256]{1,0:T(8,128)S(1)} all-reduce(f32[32,256]{1,0:T(8,128)S(1)} %fusion.20), channel_id=1, replica_groups=mesh['side'=2,'shard'=16,'tp'=8] {'tp'}, use_global_device_ids=true, to_apply=%region_6.7 | all-reduce | flops 8192 | bytes 65536 | tf_op jit(solution)/shard_map/psum | solution.py:80
  297.1 0.1 collective-permute-start
  297.2 1.2 collective-permute-done
  298.3 0.1 fusion.44
  298.5 38.0 %psum.72 = f32[32]{0:T(128)S(1)} all-reduce(f32[32]{0:T(128)S(1)} %fusion.44), channel_id=1, replica_groups=mesh['side'=2,'shard'=16,'tp'=8] {'shard'}, use_global_device_ids=true, to_apply=%region_8.9 | all-reduce | flops 32 | bytes 256 | tf_op jit(solution)/shard_map/psum | solution.py:86
  336.5 0.0 copy-start.1
  336.5 0.0 copy-start.4
  336.5 1.3 fusion.4
  337.8 0.0 all-reduce.7.cloned.1.call-update
  337.8 0.0 all-reduce.13.cloned.1.call-start
  337.8 158.1 %all-reduce.7.cloned.1.call-done = f32[32,2,1792]{2,0,1:T(8,128)} async-done(((f32[32,2,1792]{2,0,1:T(8,128)}), f32[32,2,1792]{2,0,1:T(8,128)}) %all-reduce.7.cloned.1.call-update) | async-done | bytes 458768 | tf_op jit(solution)/shard_map/psum | solution.py:90
  496.0 1.7 fusion.14
  497.6 45.9 %psum.74 = f32[32,256]{1,0:T(8,128)S(1)} all-reduce(f32[32,256]{1,0:T(8,128)S(1)} %fusion.14), channel_id=1, replica_groups=mesh['side'=2,'shard'=16,'tp'=8] {'tp'}, use_global_device_ids=true, to_apply=%region_10.11 | all-reduce | flops 8192 | bytes 65536 | tf_op jit(solution)/shard_map/psum | solution.py:93
  543.5 0.1 fusion.48
  543.6 40.8 %psum.75 = f32[32]{0:T(128)S(1)} all-reduce(f32[32]{0:T(128)S(1)} %get-tuple-element.2), channel_id=1, replica_groups=mesh['side'=2,'shard'=16,'tp'=8] {'shard'}, use_global_device_ids=true, to_apply=%region_12.13 | all-reduce | flops 32 | bytes 256 | tf_op jit(solution)/shard_map/psum | solution.py:36
  584.4 0.9 convolution_bitcast_fusion
  585.3 0.0 all-reduce.13.cloned.1.call-update
  585.3 0.0 all-reduce.9.cloned.1.call-start
  585.4 151.2 %all-reduce.13.cloned.1.call-done = f32[32,1,768]{2,0,1:T(8,128)} async-done(((f32[32,1,768]{2,0,1:T(8,128)}), f32[32,1,768]{2,0,1:T(8,128)}) %all-reduce.13.cloned.1.call-update) | async-done | bytes 98320
  736.6 0.7 constant_dynamic-slice_fusion
  737.3 0.1 subtract_convert_fusion
  737.4 0.7 fusion.117
  738.1 0.1 fusion.108
  738.3 0.1 maximum_convert_fusion.1
  738.3 0.2 multiply_reduce_fusion
  738.5 2.4 select_reduce_fusion
  740.9 0.2 fusion.30
  741.1 2.0 fusion.10
  743.2 40.1 %all_gather.7 = bf16[32,1,512]{2,1,0:T(2,128)(2,1)S(1)} all-gather(bf16[2,1,512]{2,1,0:T(2,128)(2,1)S(1)} %reshape.582), channel_id=1, replica_groups=mesh['side'=2,'shard'=16,'tp'=8] {'shard'}, dimensions={0}, use_global_device_ids=true | all-gather | bytes 34816 | tf_op jit(solution)/shard_map/all_gather | solution.py:76
  783.3 0.1 fusion.18
  783.5 45.9 %psum.76 = f32[32,256]{1,0:T(8,128)S(1)} all-reduce(f32[32,256]{1,0:T(8,128)S(1)} %fusion.18), channel_id=1, replica_groups=mesh['side'=2,'shard'=16,'tp'=8] {'tp'}, use_global_device_ids=true, to_apply=%region_17.18 | all-reduce | flops 8192 | bytes 65536 | tf_op jit(solution)/shard_map/psum | solution.py:80
  829.4 0.1 collective-permute-start.1
  829.5 1.2 collective-permute-done.1
  830.6 0.1 fusion.52
  830.8 38.0 %psum.77 = f32[32]{0:T(128)S(1)} all-reduce(f32[32]{0:T(128)S(1)} %fusion.52), channel_id=1, replica_groups=mesh['side'=2,'shard'=16,'tp'=8] {'shard'}, use_global_device_ids=true, to_apply=%region_19.20 | all-reduce | flops 32 | bytes 256 | tf_op jit(solution)/shard_map/psum | solution.py:86
  868.8 1.3 fusion.2
  870.0 0.0 all-reduce.9.cloned.1.call-update
  870.0 0.6 maximum_bitcast_fusion
  870.6 157.6 %all-reduce.9.cloned.1.call-done = f32[32,2,1792]{2,0,1:T(8,128)} async-done(((f32[32,2,1792]{2,0,1:T(8,128)}), f32[32,2,1792]{2,0,1:T(8,128)}) %all-reduce.9.cloned.1.call-update) | async-done | bytes 458768 | tf_op jit(solution)/shard_map/psum | solution.py:90
  1028.2 1.3 fusion.12
  1029.5 45.9 %psum.79 = f32[32,256]{1,0:T(8,128)S(1)} all-reduce(f32[32,256]{1,0:T(8,128)S(1)} %fusion.12), channel_id=1, replica_groups=mesh['side'=2,'shard'=16,'tp'=8] {'tp'}, use_global_device_ids=true, to_apply=%region_21.22 | all-reduce | flops 8192 | bytes 65536 | tf_op jit(solution)/shard_map/psum | solution.py:93
  1075.4 0.6 fusion.61
  (35 shorter events, 0.2 us)
Async XLA Ops:
  7.2 329.3 %copy-start = (bf16[1,256,2,1792]{3,2,1,0:T(2,128)(2,1)S(1)}, bf16[1,256,2,1792]{3,2,1,0:T(2,128)(2,1)}, u32[]{:S(2)}) copy-start(bf16[1,256,2,1792]{3,2,1,0:T(2,128)(2,1)} %param.16) | copy-start | bytes 5505028
  7.2 197.9 %all-reduce.11.cloned.1.call-start = ((), (), s32[]{:S(2)}) async-start(), calls=%async_computation.2 | async-start | bytes 196608
  55.2 440.8 %all-reduce.7.cloned.1.call-start = ((), (), s32[]{:S(2)}) async-start(), calls=%async_computation | async-start | bytes 917504 | tf_op jit(solution)/shard_map/psum | solution.py:90
  206.3 44.8 %copy-start.2 = (bf16[1,1,512,256]{3,2,1,0:T(8,128)(2,1)S(1)}, bf16[1,1,512,256]{3,2,1,0:T(8,128)(2,1)}, u32[]{:S(2)}) copy-start(bf16[1,1,512,256]{3,2,1,0:T(8,128)(2,1)} %param.14) | copy-start | bytes 786436
  206.3 90.8 %copy-start.3 = (bf16[32,256]{1,0:T(8,128)(2,1)S(1)}, bf16[32,256]{1,0:T(8,128)(2,1)}, u32[]{:S(2)}) copy-start(bf16[32,256]{1,0:T(8,128)(2,1)} %param.9) | copy-start | bytes 49156
  208.7 127.8 %copy-start.5 = (f32[1,256]{1,0:T(1,128)S(1)}, f32[1,256]{1,0:T(1,128)}, u32[]{:S(2)}) copy-start(f32[1,256]{1,0:T(1,128)} %param.15) | copy-start | bytes 3076
  297.1 1.3 collective-permute-start
  336.5 247.9 %copy-start.1 = (bf16[1,256,1,768]{3,1,2,0:T(8,128)(2,1)S(1)}, bf16[1,256,1,768]{3,1,2,0:T(8,128)(2,1)}, u32[]{:S(2)}) copy-start(bf16[1,256,1,768]{3,1,2,0:T(8,128)(2,1)} %param.13) | copy-start | bytes 1179652
  336.5 247.9 %copy-start.4 = (f32[1,256]{1,0:T(1,128)S(1)}, f32[1,256]{1,0:T(1,128)}, u32[]{:S(2)}) copy-start(f32[1,256]{1,0:T(1,128)} %param.12) | copy-start | bytes 3076
  337.8 398.8 %all-reduce.13.cloned.1.call-start = ((), (), s32[]{:S(2)}) async-start(), calls=%async_computation.3 | async-start | bytes 196608
  585.3 442.9 %all-reduce.9.cloned.1.call-start = ((), (), s32[]{:S(2)}) async-start(), calls=%async_computation.1 | async-start | bytes 917504 | tf_op jit(solution)/shard_map/psum | solution.py:90
  743.2 285.1 %copy-start.6 = (bf16[1,1792,256]{2,1,0:T(8,128)(2,1)S(1)}, bf16[1,1792,256]{2,1,0:T(8,128)(2,1)}, u32[]{:S(2)}) copy-start(bf16[1,1792,256]{2,1,0:T(8,128)(2,1)} %param.17) | copy-start | bytes 2752516
  829.4 1.3 collective-permute-start.1
Sparse Core Ops, SparseCore 0:
  55.3 149.7 all-reduce.10
  337.9 158.0 all-reduce.6
  585.4 151.0 all-reduce.12
  870.2 158.0 all-reduce.8
where the time goes:
time: 1090 us; the launch traced here: 1080 us
  waiting for transfers between devices  616 us (57%)
  blocking collectives  426 us (39%)
  matrix products  17.3 us (2%)
  between operations  14.6 us (1%)
    psum x2, waiting for transfers between devices, feed_forward(): both_terms = lax.psum(both_terms, 'shard')  316 us
    unnamed x6, waiting for transfers between devices  298 us
    psum x2, blocking collectives, feed_forward(): summed = lax.psum(partial_out, 'tp')  91.8 us
    psum x2, blocking collectives, attend(): projected = lax.psum(projected, 'tp')  91.8 us
    psum x2, blocking collectives, attend(): square_sum = lax.psum(jnp.sum(values_f32 * values_f32, axis=1), 'shard')  85.8 us
    all_gather x2, blocking collectives, attend(): lax.all_gather(attended, 'shard', axis=0, tiled=True)  80.2 us
    psum x2, blocking collectives, feed_forward(): square_sum = lax.psum(jnp.sum(values_f32 * values_f32, axis=1), 'shard')  76 us
  transfers between devices with their start and end apart: 6, of which 6 were waited for; matrix products, arithmetic and copies ran while one was open for 0% of the time, Pallas kernels for 0%

commit v1 on v0

v1 whole, which is shorter than its diff:
```python
import functools

import jax
import jax.numpy as jnp
import numpy as np
from jax import lax
from jax.experimental import pallas as pl
from jax.experimental.pallas import tpu as pltpu
from jax.sharding import PartitionSpec as P

D = 4096
HD = 128
ROWS = 32
EPSILON = 1e-05
ROPE_BASE = 500000.0
SHARDS = 16
TPS = 8
TILES = 14
CTX = 4096
BF = jnp.bfloat16
F32 = jnp.float32


def nt_dot(a, b):
    return lax.dot_general(a, b, (((1,), (1,)), ((), ())), preferred_element_type=F32)


def wait_bytes(ref, sem):
    pltpu.make_async_copy(ref, ref, sem).wait()


def kernel(
    tok_ref, lens_ref, again_ref, fgain_ref, freq_ref, cache_hbm, wqkv_hbm, wout_hbm, wgu_hbm, wdn_hbm,
    out_ref, scale_ref,
    kbuf, vbuf, wqkv, wout, graw, wgu, wdn,
    x_buf, a_buf, resid,
    ss_send, ss_recv, stage, send1, recv1, send2, recv2, heads_f32,
    send3, recv3, send4, recv4, send5, recv5, send6, recv6,
    load_sem, gu_sem, ss_send_sem, ss_recv_sem, send_sem, recv_sem, res_sem,
):
    side = lax.axis_index("side")
    s = lax.axis_index("shard")
    t = lax.axis_index("tp")

    def shard_peer(d):
        return lax.rem(s + d, SHARDS)

    def tp_peer(d):
        return lax.rem(t + d, TPS)

    def remote(src, dst, ssem, rsem, device):
        return pltpu.make_async_remote_copy(
            src_ref=src, dst_ref=dst, send_sem=ssem, recv_sem=rsem, device_id=device,
            device_id_type=pl.DeviceIdType.MESH,
        )

    loads = [pltpu.make_async_copy(wqkv_hbm, wqkv, load_sem.at[0])]
    for i in range(2):
        loads.append(pltpu.make_async_copy(
            cache_hbm.at[i, :, pl.ds(0, HD)], kbuf.at[:, pl.ds(HD * i, HD)], load_sem.at[1 + i]))
        loads.append(pltpu.make_async_copy(
            cache_hbm.at[i, :, pl.ds(HD, HD)], vbuf.at[:, pl.ds(HD * i, HD)], load_sem.at[3 + i]))
    loads.append(pltpu.make_async_copy(wout_hbm, wout, load_sem.at[5]))
    loads.append(pltpu.make_async_copy(wdn_hbm, wdn, load_sem.at[6]))
    for load in loads:
        load.start()
    gu_loads = [
        pltpu.make_async_copy(wgu_hbm.at[:, :, pl.ds(HD * j, HD)], graw.at[j], gu_sem.at[j]) for j in range(TILES)
    ]
    for load in gu_loads:
        load.start()

    barrier = pltpu.get_barrier_semaphore()

    def greet(device):
        pl.semaphore_signal(barrier, inc=1, device_id=device, device_id_type=pl.DeviceIdType.MESH)

    def greet_shard(d, carry):
        greet((side, shard_peer(d), t))
        return carry

    def greet_tp(d, carry):
        greet((side, s, tp_peer(d)))
        return carry

    def greet_other(d, carry):
        greet((1 - side, s, tp_peer(d)))
        return carry

    lax.fori_loop(1, SHARDS, greet_shard, 0)
    lax.fori_loop(1, TPS, greet_tp, 0)
    lax.fori_loop(0, TPS, greet_other, 0)

    stage[...] = jnp.zeros_like(stage)
    x_buf[...] = tok_ref[...]
    diagonal = lax.broadcasted_iota(jnp.int32, (ROWS, HD), 0) == lax.broadcasted_iota(jnp.int32, (ROWS, HD), 1)
    pl.semaphore_wait(barrier, SHARDS - 1 + 2 * TPS - 1)

    def share_squares(values, which):
        column = jnp.sum(values * values, axis=1, keepdims=True)
        row = jnp.sum(jnp.where(diagonal, column, 0.0), axis=0, keepdims=True)
        ss_send[which] = row
        ss_recv[which, s] = row

        def go(d, carry):
            remote(ss_send.at[which], ss_recv.at[which, s], ss_send_sem.at[which], ss_recv_sem.at[which],
                   (side, shard_peer(d), t)).start()
            return carry

        lax.fori_loop(1, SHARDS, go, 0)

    def squares_factor(which):
        wait_bytes(ss_recv.at[which, pl.ds(0, SHARDS - 1)], ss_recv_sem.at[which])
        total = jnp.sum(ss_recv[which], axis=0)
        factor = lax.rsqrt(total / D + EPSILON)
        scale_ref[pl.ds(which, 1), :] = factor[:, :ROWS]
        return factor

    def attention():
        values = x_buf[...].astype(F32)
        share_squares(values, 0)
        scaled = (values * again_ref[...]).astype(BF)
        loads[0].wait()
        mixed = jnp.dot(scaled, wqkv[...], preferred_element_type=F32)
        for part in range(6):
            stage[pl.ds(part, ROWS, stride=8), :] = mixed[:, HD * part:HD * (part + 1)]
        send1[...] = stage[...].astype(BF)
        recv1[s] = send1[pl.ds(pl.multiple_of(16 * s, 16), 16), :]

        def go1(d, carry):
            to = shard_peer(d)
            remote(send1.at[pl.ds(pl.multiple_of(16 * to, 16), 16)], recv1.at[s], send_sem.at[0], recv_sem.at[0],
                   (side, to, t)).start()
            return carry

        lax.fori_loop(1, SHARDS, go1, 0)

        lens = [lens_ref[2 * s + i] for i in range(2)]
        lane = lax.broadcasted_iota(jnp.int32, (1, HD), 1)
        upper_row = lax.broadcasted_iota(jnp.int32, (16, 1), 0) >= 8
        position = jnp.where(upper_row, lens[1], lens[0])
        angle = position.astype(F32) * freq_ref[...]
        cosine = jnp.cos(angle)
        sine = jnp.where(lane < HD // 2, -jnp.sin(angle), jnp.sin(angle))

        factor = squares_factor(0)
        own_factor = jnp.sum(
            jnp.where(lane == jnp.where(upper_row, 2 * s + 1, 2 * s), factor, 0.0), axis=1, keepdims=True)
        wait_bytes(recv1.at[pl.ds(0, SHARDS - 1)], recv_sem.at[0])
        own = jnp.sum(recv1[...].astype(F32), axis=0) * own_factor
        rotated = own * cosine + pltpu.roll(own, HD // 2, 1) * sine
        rotated = rotated.astype(BF).astype(F32)
        own_values = own.astype(BF).astype(F32)
        new_key = jnp.concatenate(
            [jnp.broadcast_to(rotated[8 * i + 4:8 * i + 5], (8, HD)) for i in range(2)], axis=0)
        new_value = jnp.concatenate(
            [jnp.broadcast_to(own_values[8 * i + 5:8 * i + 6], (8, HD)) for i in range(2)], axis=0)
        own_score = jnp.sum(rotated * new_key, axis=1, keepdims=True) * HD ** (-0.5)
        both = jnp.concatenate(
            [jnp.where(upper_row, 0.0, rotated), jnp.where(upper_row, rotated, 0.0)], axis=1).astype(BF)
        loads[1].wait()
        loads[3].wait()
        scores = nt_dot(both, kbuf[...]) * HD ** (-0.5)
        at = lax.broadcasted_iota(jnp.int32, (16, CTX), 1)
        scores = jnp.where(at < position, scores, -1e30)
        top = jnp.maximum(jnp.max(scores, axis=1, keepdims=True), own_score)
        weights = jnp.exp(scores - top)
        own_weight = jnp.exp(own_score - top)
        total = jnp.sum(weights, axis=1, keepdims=True) + own_weight
        loads[2].wait()
        loads[4].wait()
        mixed_values = jnp.dot(weights.astype(BF), vbuf[...], preferred_element_type=F32)
        mixed_values = jnp.concatenate([mixed_values[:8, :HD], mixed_values[8:, HD:]], axis=0)
        mixed_values = mixed_values + own_weight.astype(BF).astype(F32) * new_value
        heads = (mixed_values / total).astype(BF)
        send2[...] = heads
        recv2[s] = heads

        def go2(d, carry):
            remote(send2, recv2.at[s], send_sem.at[1], recv_sem.at[1], (side, shard_peer(d), t)).start()
            return carry

        lax.fori_loop(1, SHARDS, go2, 0)
        loads[5].wait()
        wait_bytes(recv2.at[pl.ds(0, SHARDS - 1)], recv_sem.at[1])
        heads_f32[...] = recv2[...].astype(F32).reshape(16 * SHARDS, HD)
        gathered = jnp.concatenate(
            [heads_f32[pl.ds(g, ROWS, stride=8), :] for g in range(4)], axis=1).astype(BF)
        send3[...] = jnp.dot(gathered, wout[...], preferred_element_type=F32).astype(BF)

        def go3(d, carry):
            remote(send3, recv3.at[t], send_sem.at[2], recv_sem.at[2], (1 - side, s, tp_peer(d))).start()
            return carry

        lax.fori_loop(0, TPS, go3, 0)

    def prepare():
        for load in gu_loads:
            load.wait()
        out_row = lax.broadcasted_iota(jnp.int32, (512, 512), 0)
        in_row = lax.broadcasted_iota(jnp.int32, (512, 512), 1)
        wanted = jnp.where(out_row < 256, 2 * out_row, 2 * (out_row - 256) + 1)
        pick = jnp.where(in_row == wanted, 1.0, 0.0).astype(BF)

        def one(j, carry):
            apart = jnp.dot(pick, graw[j].reshape(512, HD), preferred_element_type=F32).astype(BF)
            wgu[j] = jnp.concatenate([apart[:256], apart[256:]], axis=1)
            return carry

        lax.fori_loop(0, TILES, one, 0)

    def feed_forward():
        prepare()

        @pl.when(side == 1)
        def _():
            resid[...] = tok_ref[...]

        @pl.when(side == 0)
        def _():
            wait_bytes(resid, res_sem.at[1])

        wait_bytes(recv3, recv_sem.at[2])
        after = (resid[...].astype(F32) + jnp.sum(recv3[...].astype(F32), axis=0)).astype(BF)
        a_buf[...] = after
        values = after.astype(F32)
        share_squares(values, 1)
        scaled = (values * fgain_ref[...]).astype(BF)

        def tile(j, carry):
            send4[j] = jnp.dot(scaled, wgu[j], preferred_element_type=F32).astype(BF)
            return carry

        lax.fori_loop(0, TILES, tile, 0)

        @pl.when(s < TILES)
        def _():
            recv4[s] = send4[s]

        def go4(d, carry):
            to = shard_peer(d)

            @pl.when(to < TILES)
            def _():
                remote(send4.at[to], recv4.at[s], send_sem.at[3], recv_sem.at[3], (side, to, t)).start()

            return carry

        lax.fori_loop(1, SHARDS, go4, 0)
        factor = squares_factor(1)
        column = jnp.sum(jnp.where(diagonal, factor, 0.0), axis=1, keepdims=True)

        @pl.when(s < TILES)
        def _():
            wait_bytes(recv4.at[pl.ds(0, SHARDS - 1)], recv_sem.at[3])
            both = jnp.sum(recv4[...].astype(F32), axis=0) * column
            gate, up = both[:, :HD], both[:, HD:]
            hidden = (gate / (1.0 + jnp.exp(-gate)) * up).astype(BF)
            send5[...] = hidden
            recv5[s] = hidden

            def go5(d, carry):
                remote(send5, recv5.at[s], send_sem.at[4], recv_sem.at[4], (side, shard_peer(d), t)).start()
                return carry

            lax.fori_loop(1, SHARDS, go5, 0)

        loads[6].wait()

        @pl.when(s < TILES)
        def _():
            wait_bytes(recv5.at[pl.ds(0, TILES - 1)], recv_sem.at[4])

        @pl.when(s >= TILES)
        def _():
            wait_bytes(recv5, recv_sem.at[4])

        hidden_all = jnp.concatenate([recv5[j] for j in range(TILES)], axis=1)
        partial = jnp.dot(hidden_all, wdn[...], preferred_element_type=F32).astype(BF)
        send6[...] = partial
        recv6[t] = partial

        def go6(d, carry):
            remote(send6, recv6.at[t], send_sem.at[5], recv_sem.at[5], (side, s, tp_peer(d))).start()
            return carry

        lax.fori_loop(1, TPS, go6, 0)
        wait_bytes(recv6.at[pl.ds(0, TPS - 1)], recv_sem.at[5])
        result = (a_buf[...].astype(F32) + jnp.sum(recv6[...].astype(F32), axis=0)).astype(BF)
        out_ref[...] = result

        @pl.when(side == 1)
        def _():
            x_buf[...] = result
            remote(x_buf, resid, res_sem.at[0], res_sem.at[1], (0, s, t)).start()

    pl.when(side == 0)(attention)
    feed_forward()
    pl.when(side == 1)(attention)

    for which in range(2):
        wait_bytes(ss_recv.at[which, pl.ds(0, SHARDS - 1)], ss_send_sem.at[which])
    wait_bytes(recv1.at[pl.ds(0, SHARDS - 1)], send_sem.at[0])
    wait_bytes(recv2.at[pl.ds(0, SHARDS - 1)], send_sem.at[1])
    wait_bytes(recv3, send_sem.at[2])

    @pl.when(s < TILES)
    def _():
        wait_bytes(recv4.at[pl.ds(0, TILES - 1)], send_sem.at[3])
        wait_bytes(recv2_like(recv5_full=recv4, rows=SHARDS - 1), send_sem.at[4])

    @pl.when(s >= TILES)
    def _():
        wait_bytes(recv4.at[pl.ds(0, TILES)], send_sem.at[3])

    wait_bytes(recv6.at[pl.ds(0, TPS - 1)], send_sem.at[5])

    @pl.when(side == 1)
    def _():
        wait_bytes(x_buf, res_sem.at[0])


def recv2_like(recv5_full, rows):
    return recv5_full.at[pl.ds(0, rows), :, pl.ds(0, HD)]


def body(tokens, lengths, kv_cache, attn_gain, qkv_weight, out_weight, ffn_gain, gate_up, down_weight):
    freqs = (ROPE_BASE ** (-np.arange(HD // 2, dtype=np.float64) * 2.0 / HD)).astype(np.float32)
    freqs = jnp.asarray(np.concatenate([freqs, freqs])[None])
    vmem = pl.BlockSpec(memory_space=pltpu.VMEM)
    smem = pl.BlockSpec(memory_space=pltpu.SMEM)
    hbm = pl.BlockSpec(memory_space=pl.ANY)
    out, scales = pl.pallas_call(
        kernel,
        out_shape=(jax.ShapeDtypeStruct((ROWS, 256), BF), jax.ShapeDtypeStruct((2, ROWS), F32)),
        in_specs=[vmem, smem, vmem, vmem, vmem, hbm, hbm, hbm, hbm, hbm],
        out_specs=(vmem, vmem),
        scratch_shapes=[
            pltpu.VMEM((CTX, 2 * HD), BF), pltpu.VMEM((CTX, 2 * HD), BF),
            pltpu.VMEM((256, 768), BF), pltpu.VMEM((512, 256), BF),
            pltpu.VMEM((TILES, 256, 2, HD), BF), pltpu.VMEM((TILES, 256, 2 * HD), BF),
            pltpu.VMEM((TILES * HD, 256), BF),
            pltpu.VMEM((ROWS, 256), BF), pltpu.VMEM((ROWS, 256), BF), pltpu.VMEM((ROWS, 256), BF),
            pltpu.VMEM((2, 1, HD), F32), pltpu.VMEM((2, SHARDS, 1, HD), F32),
            pltpu.VMEM((16 * SHARDS, HD), F32), pltpu.VMEM((16 * SHARDS, HD), BF),
            pltpu.VMEM((SHARDS, 16, HD), BF),
            pltpu.VMEM((16, HD), BF), pltpu.VMEM((SHARDS, 16, HD), BF), pltpu.VMEM((16 * SHARDS, HD), F32),
            pltpu.VMEM((ROWS, 256), BF), pltpu.VMEM((TPS, ROWS, 256), BF),
            pltpu.VMEM((TILES, ROWS, 256), BF), pltpu.VMEM((SHARDS, ROWS, 256), BF),
            pltpu.VMEM((ROWS, HD), BF), pltpu.VMEM((TILES, ROWS, HD), BF),
            pltpu.VMEM((ROWS, 256), BF), pltpu.VMEM((TPS, ROWS, 256), BF),
            pltpu.SemaphoreType.DMA((7,)), pltpu.SemaphoreType.DMA((TILES,)),
            pltpu.SemaphoreType.DMA((2,)), pltpu.SemaphoreType.DMA((2,)),
            pltpu.SemaphoreType.DMA((6,)), pltpu.SemaphoreType.DMA((6,)), pltpu.SemaphoreType.DMA((2,)),
        ],
        compiler_params=pltpu.CompilerParams(
            collective_id=0, has_side_effects=True, vmem_limit_bytes=48 * 1024 * 1024),
        cost_estimate=pl.CostEstimate(flops=130_000_000, bytes_accessed=7_500_000, transcendentals=70_000),
    )(
        tokens, lengths, attn_gain, ffn_gain, freqs,
        kv_cache.reshape(2, CTX, 2 * HD), qkv_weight.reshape(256, 768), out_weight.reshape(512, 256),
        gate_up.reshape(256, 2, 1792), down_weight.reshape(1792, 256),
    )
    return (out[None], scales[None])


def solution(mesh):
    in_specs = (
        P(None, "shard"),
        P(),
        P("side", "shard", None, "tp", None),
        P("side", "shard"),
        P("side", "shard", "tp", None),
        P("side", "tp", None, "shard"),
        P("side", "shard"),
        P("side", "shard", None, "tp"),
        P("side", "tp", "shard"),
    )
    out_specs = (P("side", None, "shard"), P("side", None, None))
    return jax.shard_map(body, mesh=mesh, in_specs=in_specs, out_specs=out_specs, check_vma=False)
```

time: 1090 us -> 95.2 us (0.09)
  waiting for transfers between devices: 616 us -> 0 us
  blocking collectives: 426 us -> 0 us
  Pallas kernels: 0 us -> 84.6 us
  matrix products: 17.3 us -> 0 us
  between operations: 14.6 us -> 0.66 us
    psum x8 -> x0, blocking collectives: 345 us -> none  [the longest x2 91.8 us: feed_forward(): summed = lax.psum(partial_out, 'tp')]
    psum x2 -> x0, waiting for transfers between devices: 316 us -> none  [feed_forward(): both_terms = lax.psum(both_terms, 'shard')]
    unnamed x6 -> x0, waiting for transfers between devices: 298 us -> none
    pallas_call x0 -> x1, Pallas kernels: none -> 84.6 us  [body(): pl.pallas_call(kernel, out_shape=(jax.ShapeDtypeStruct((ROWS, 256), BF),...]
    all_gather x2 -> x0, blocking collectives: 80.2 us -> none  [attend(): lax.all_gather(attended, 'shard', axis=0, tiled=True)]
    dot_general x12 -> x0, matrix products: 17.3 us -> none  [the longest x2 4.77 us: attend(): jnp.einsum('rkgh,rtkh->rkgt', queries, own_cache[..., :HD], preferred_ele...]
  transfers between devices with their start and end apart: 6 -> 0, of which waited for: 6 -> 0; matrix products, arithmetic and copies ran while one was open for 0% -> 0% of each run, Pallas kernels for 0% -> 0%
where the time goes in v1:
time: 95.2 us; the launch traced here: 94.4 us
  Pallas kernels  84.6 us (89%)
  local copies, waits for them, and re-layouts  9.17 us (10%)
    pallas_call x1, Pallas kernels, body(): pl.pallas_call(kernel, out_shape=(jax.ShapeDtypeStruct((ROWS, 256), BF),...  84.6 us
    unnamed x20, local copies, waits for them, and re-layouts  9.17 us

profile of v1, /device:TPU:6, one launch (start us, length us, event | category | flops | bytes accessed | tf_op | source)
XLA Modules:
  0.0 94.4 jit_solution(15907837139335863532)
XLA Ops:
  0.6 0.0 copy-start
  0.6 1.5 %copy-done = bf16[1,256,2,1792]{3,2,1,0:T(2,128)(2,1)S(1)} copy-done((bf16[1,256,2,1792]{3,2,1,0:T(2,128)(2,1)S(1)}, bf16[1,256,2,1792]{3,2,1,0:T(2,128)(2,1)}, u32[]{:S(2)}) %copy-start) | copy-done | bytes 1835032
  2.1 0.0 copy-start.1
  2.1 1.2 %copy-done.1 = bf16[1,1792,256]{2,1,0:T(8,128)(2,1)S(1)} copy-done((bf16[1,1792,256]{2,1,0:T(8,128)(2,1)S(1)}, bf16[1,1792,256]{2,1,0:T(8,128)(2,1)}, u32[]{:S(2)}) %copy-start.1) | copy-done | bytes 917528
  3.3 0.0 copy-start.2
  3.3 1.0 %copy-done.2 = bf16[1,256,1,768]{3,1,2,0:T(8,128)(2,1)S(1)} copy-done((bf16[1,256,1,768]{3,1,2,0:T(8,128)(2,1)S(1)}, bf16[1,256,1,768]{3,1,2,0:T(8,128)(2,1)}, u32[]{:S(2)}) %copy-start.2) | copy-done | bytes 393240
  4.3 0.0 copy-start.3
  4.3 0.9 %copy-done.3 = bf16[1,1,512,256]{3,2,1,0:T(8,128)(2,1)S(1)} copy-done((bf16[1,1,512,256]{3,2,1,0:T(8,128)(2,1)S(1)}, bf16[1,1,512,256]{3,2,1,0:T(8,128)(2,1)}, u32[]{:S(2)}) %copy-start.3) | copy-done | bytes 262168
  5.3 0.0 copy-start.4
  5.3 0.7 copy-done.4
  6.0 0.0 copy-start.5
  6.0 0.7 copy-done.5
  6.7 0.0 copy-start.6
  6.7 0.7 copy-done.6
  7.3 0.0 copy-start.7
  7.3 0.7 copy-done.7
  8.0 0.0 copy-start.8
  8.0 0.7 copy-done.8
  8.6 84.6 %shard_map.113 = (bf16[32,256]{1,0:T(8,128)(2,1)S(1)}, f32[2,32]{1,0:T(2,128)S(1)}) custom-call(bf16[32,256]{1,0:T(8,128)(2,1)S(1)} %copy-done.4, s32[32]{0:T(128)S(1)} %copy-done.7, f32[1,256]{1,0:T(1,128)S(1)} %copy-done.5, f32[1,256]{1,0:T(1,128)S(1)} %copy-done.6, f32[1,128]{1,0:T(1,128)S(1)} %copy-done.8, bf16[2,4096,256]{2,1,0:T(8,128)(2,1)} %bitcast.13, ...), custom_call_target="tpu_custom_call" | custom-call | flops 130000000 | bytes 7500000 | tf_op jit(solution)/shard_map/pallas_call | solution.py:333
  93.3 0.6 copy.14
  93.9 0.6 copy.15
Async XLA Ops:
  0.6 1.5 %copy-start = (bf16[1,256,2,1792]{3,2,1,0:T(2,128)(2,1)S(1)}, bf16[1,256,2,1792]{3,2,1,0:T(2,128)(2,1)}, u32[]{:S(2)}) copy-start(bf16[1,256,2,1792]{3,2,1,0:T(2,128)(2,1)} %param.17) | copy-start | bytes 5505028
  2.1 1.2 %copy-start.1 = (bf16[1,1792,256]{2,1,0:T(8,128)(2,1)S(1)}, bf16[1,1792,256]{2,1,0:T(8,128)(2,1)}, u32[]{:S(2)}) copy-start(bf16[1,1792,256]{2,1,0:T(8,128)(2,1)} %param.18) | copy-start | bytes 2752516
  3.3 1.0 %copy-start.2 = (bf16[1,256,1,768]{3,1,2,0:T(8,128)(2,1)S(1)}, bf16[1,256,1,768]{3,1,2,0:T(8,128)(2,1)}, u32[]{:S(2)}) copy-start(bf16[1,256,1,768]{3,1,2,0:T(8,128)(2,1)} %param.14) | copy-start | bytes 1179652
  4.3 0.9 %copy-start.3 = (bf16[1,1,512,256]{3,2,1,0:T(8,128)(2,1)S(1)}, bf16[1,1,512,256]{3,2,1,0:T(8,128)(2,1)}, u32[]{:S(2)}) copy-start(bf16[1,1,512,256]{3,2,1,0:T(8,128)(2,1)} %param.15) | copy-start | bytes 786436
  5.3 0.7 copy-start.4
  6.0 0.7 copy-start.5
  6.7 0.7 copy-start.6
  7.3 0.7 copy-start.7
  8.0 0.7 copy-start.8

commit v2 on v1

v2 whole, which is shorter than its diff:
```python
import jax
import jax.numpy as jnp
import numpy as np
from jax import lax
from jax.experimental import pallas as pl
from jax.experimental.pallas import tpu as pltpu
from jax.sharding import PartitionSpec as P

D = 4096
HD = 128
ROWS = 32
EPSILON = 1e-05
ROPE_BASE = 500000.0
SHARDS = 16
TPS = 8
TILES = 14
OWNERS = 7
CTX = 4096
BF = jnp.bfloat16
F32 = jnp.float32
MESH = pl.DeviceIdType.MESH


def nt_dot(a, b):
    return lax.dot_general(a, b, (((1,), (1,)), ((), ())), preferred_element_type=F32)


def wait_bytes(ref, sem):
    pltpu.make_async_copy(ref, ref, sem).wait()


def remote(src, dst, ssem, rsem, device):
    return pltpu.make_async_remote_copy(
        src_ref=src, dst_ref=dst, send_sem=ssem, recv_sem=rsem, device_id=device, device_id_type=MESH)


def kernel(
    tok_hbm, lens_hbm, again_hbm, fgain_hbm, freq_hbm, cache_hbm, wqkv_hbm, wout_hbm, wgu_hbm, wdn_hbm,
    out_ref, scale_ref,
    lens, again, fgain, freq,
    kbuf, vbuf, wqkv, wout, graw, wgu, wdn,
    x_buf, a_buf,
    ss_send, ss_recv, stage, send1, recv1, send2, recv2, heads_f32,
    send3, recv3, send4, recv4, send5, recv5, send6, recv6, end_buf, end_scale,
    load_sem, gu_sem, ss_send_sem, ss_recv_sem, send1_sem, recv1_sem, send2_sem, recv2_sem,
    send_sem, recv_sem, push_send, push_recv, end_send, end_recv,
):
    side = lax.axis_index("side")
    s = lax.axis_index("shard")
    t = lax.axis_index("tp")
    mate = (1 - side, s, t)

    def shard_peer(d):
        return lax.rem(s + d, SHARDS)

    def tp_peer(d):
        return lax.rem(t + d, TPS)

    barrier = pltpu.get_barrier_semaphore()

    def greet(device):
        pl.semaphore_signal(barrier, inc=1, device_id=device, device_id_type=MESH)

    def loop(start, stop, step):
        def go(d, carry):
            step(d)
            return carry

        lax.fori_loop(start, stop, go, 0)

    @pl.when(side == 0)
    def _():
        loop(1, SHARDS, lambda d: greet((0, shard_peer(d), t)))
        greet(mate)

    @pl.when(side == 1)
    def _():
        loop(0, SHARDS, lambda d: greet((0, shard_peer(d), t)))
        loop(1, SHARDS, lambda d: greet((1, shard_peer(d), t)))
        loop(1, TPS, lambda d: greet((1, s, tp_peer(d))))

    first_loads = [
        pltpu.make_async_copy(tok_hbm, x_buf, load_sem.at[0]),
        pltpu.make_async_copy(again_hbm, again, load_sem.at[1]),
        pltpu.make_async_copy(wqkv_hbm, wqkv, load_sem.at[2]),
        pltpu.make_async_copy(lens_hbm, lens, load_sem.at[3]),
        pltpu.make_async_copy(freq_hbm, freq, load_sem.at[4]),
    ]
    cache_loads = []
    for i in range(2):
        cache_loads.append(pltpu.make_async_copy(
            cache_hbm.at[i, :, pl.ds(0, HD)], kbuf.at[:, pl.ds(HD * i, HD)], load_sem.at[5 + i]))
        cache_loads.append(pltpu.make_async_copy(
            cache_hbm.at[i, :, pl.ds(HD, HD)], vbuf.at[:, pl.ds(HD * i, HD)], load_sem.at[7 + i]))
    own_loads = [
        pltpu.make_async_copy(fgain_hbm, fgain.at[0], load_sem.at[9]),
        pltpu.make_async_copy(wdn_hbm, wdn.at[0], load_sem.at[10]),
        pltpu.make_async_copy(wout_hbm, wout.at[1], load_sem.at[11]),
    ]
    gu_loads = [
        pltpu.make_async_copy(wgu_hbm.at[:, :, pl.ds(HD * j, HD)], graw.at[j], gu_sem.at[j]) for j in range(TILES)
    ]
    for load in first_loads:
        load.start()

    @pl.when(side == 0)
    def _():
        for load in cache_loads:
            load.start()

    for load in gu_loads:
        load.start()

    @pl.when(side == 1)
    def _():
        for load in own_loads:
            load.start()
        for load in cache_loads:
            load.start()

    pushes = [
        remote(wout_hbm, wout.at[0], push_send.at[0], push_recv.at[0], mate),
        remote(fgain_hbm, fgain.at[1], push_send.at[1], push_recv.at[1], mate),
        remote(wdn_hbm, wdn.at[1], push_send.at[2], push_recv.at[2], mate),
        remote(wgu.at[1], wgu.at[1], push_send.at[3], push_recv.at[3], mate),
    ]

    stage[...] = jnp.zeros_like(stage)
    diagonal = lax.broadcasted_iota(jnp.int32, (ROWS, HD), 0) == lax.broadcasted_iota(jnp.int32, (ROWS, HD), 1)
    lane = lax.broadcasted_iota(jnp.int32, (1, HD), 1)

    def put_squares(values, which):
        column = jnp.sum(values * values, axis=1, keepdims=True)
        row = jnp.sum(jnp.where(diagonal, column, 0.0), axis=0, keepdims=True)
        ss_send[which] = row
        ss_recv[which, s] = row

    def send_squares(which, d):
        remote(ss_send.at[which], ss_recv.at[which, s], ss_send_sem.at[which], ss_recv_sem.at[which],
               (side, shard_peer(d), t)).start()

    def squares_factor(which):
        wait_bytes(ss_recv.at[which, pl.ds(0, SHARDS - 1)], ss_recv_sem.at[which])
        return lax.rsqrt(jnp.sum(ss_recv[which], axis=0) / D + EPSILON)

    def attention():
        @pl.when(side == 0)
        def _():
            first_loads[0].wait()
            first_loads[1].wait()
            first_loads[2].wait()

        values = x_buf[...].astype(F32)
        put_squares(values, 2)
        mixed = jnp.dot((values * again[...]).astype(BF), wqkv[...], preferred_element_type=F32)
        for part in range(6):
            stage[pl.ds(part, ROWS, stride=8), :] = mixed[:, HD * part:HD * (part + 1)]
        send1[...] = stage[...].astype(BF).reshape(SHARDS, 16, HD)
        recv1[s] = send1[s]

        @pl.when(side == 0)
        def _():
            pl.semaphore_wait(barrier, 2 * SHARDS - 1)

        def go1(d):
            to = shard_peer(d)
            send_squares(2, d)
            remote(send1.at[to], recv1.at[s], send1_sem, recv1_sem, (side, to, t)).start()

        loop(1, SHARDS, go1)

        @pl.when(side == 0)
        def _():
            pushes[0].start()
            first_loads[3].wait()
            first_loads[4].wait()

        lens_here = [lens[2 * s + i] for i in range(2)]
        upper_row = lax.broadcasted_iota(jnp.int32, (16, 1), 0) >= 8
        position = jnp.where(upper_row, lens_here[1], lens_here[0])
        angle = position.astype(F32) * freq[...]
        cosine = jnp.cos(angle)
        sine = jnp.where(lane < HD // 2, -jnp.sin(angle), jnp.sin(angle))

        factor = squares_factor(2)
        scale_ref[0:1, :] = factor[:, :ROWS]
        own_factor = jnp.sum(
            jnp.where(lane == jnp.where(upper_row, 2 * s + 1, 2 * s), factor, 0.0), axis=1, keepdims=True)
        wait_bytes(recv1.at[pl.ds(0, SHARDS - 1)], recv1_sem)
        own = jnp.sum(recv1[...].astype(F32), axis=0) * own_factor
        rotated = own * cosine + pltpu.roll(own, HD // 2, 1) * sine
        rotated = rotated.astype(BF).astype(F32)
        own_values = own.astype(BF).astype(F32)
        new_key = jnp.concatenate(
            [jnp.broadcast_to(rotated[8 * i + 4:8 * i + 5], (8, HD)) for i in range(2)], axis=0)
        new_value = jnp.concatenate(
            [jnp.broadcast_to(own_values[8 * i + 5:8 * i + 6], (8, HD)) for i in range(2)], axis=0)
        own_score = jnp.sum(rotated * new_key, axis=1, keepdims=True) * HD ** (-0.5)
        both = jnp.concatenate(
            [jnp.where(upper_row, 0.0, rotated), jnp.where(upper_row, rotated, 0.0)], axis=1).astype(BF)

        @pl.when(side == 0)
        def _():
            for load in cache_loads:
                load.wait()

        scores = nt_dot(both, kbuf[...]) * HD ** (-0.5)
        at = lax.broadcasted_iota(jnp.int32, (16, CTX), 1)
        scores = jnp.where(at < position, scores, -1e30)
        top = jnp.maximum(jnp.max(scores, axis=1, keepdims=True), own_score)
        weights = jnp.exp(scores - top)
        own_weight = jnp.exp(own_score - top)
        total = jnp.sum(weights, axis=1, keepdims=True) + own_weight
        mixed_values = jnp.dot(weights.astype(BF), vbuf[...], preferred_element_type=F32)
        mixed_values = jnp.concatenate([mixed_values[:8, :HD], mixed_values[8:, HD:]], axis=0)
        mixed_values = mixed_values + own_weight.astype(BF).astype(F32) * new_value
        heads = (mixed_values / total).astype(BF)
        send2[...] = heads

        @pl.when(side == 1)
        def _():
            recv2[1, s] = heads

        @pl.when(side == 0)
        def _():
            remote(send2, recv2.at[side, s], send2_sem, recv2_sem.at[side], mate).start()

        loop(1, SHARDS, lambda d: remote(
            send2, recv2.at[side, s], send2_sem, recv2_sem.at[side], (1, shard_peer(d), t)).start())

    def prepare(slot):
        for load in gu_loads:
            load.wait()
        out_row = lax.broadcasted_iota(jnp.int32, (512, 512), 0)
        in_row = lax.broadcasted_iota(jnp.int32, (512, 512), 1)
        wanted = jnp.where(out_row < 256, 2 * out_row, 2 * (out_row - 256) + 1)
        pick = jnp.where(in_row == wanted, 1.0, 0.0).astype(BF)

        def one(o):
            for half in range(2):
                apart = jnp.dot(pick, graw[2 * o + half].reshape(512, HD), preferred_element_type=F32).astype(BF)
                wgu[slot, o, :, HD * half:HD * (half + 1)] = apart[:256]
                wgu[slot, o, :, 256 + HD * half:256 + HD * (half + 1)] = apart[256:]

        loop(0, OWNERS, one)

    owner = 2 * (s // 4) + s % 4 - 1
    owns = (s % 4 >= 1) & (s % 4 <= 2) & (owner < OWNERS)

    def layer(l):
        @pl.when(l == 0)
        def _():
            wait_bytes(wout.at[0], push_recv.at[0])
            wait_bytes(recv2.at[0], recv2_sem.at[0])

        @pl.when(l == 1)
        def _():
            own_loads[2].wait()
            wait_bytes(recv2.at[1, pl.ds(0, SHARDS - 1)], recv2_sem.at[1])

        heads_f32[...] = recv2[l].astype(F32).reshape(16 * SHARDS, HD)
        gathered = jnp.concatenate(
            [heads_f32[pl.ds(g, ROWS, stride=8), :] for g in range(4)], axis=1).astype(BF)
        projected = jnp.dot(gathered, wout[l], preferred_element_type=F32).astype(BF)
        send3[l] = projected
        recv3[l, t] = projected
        loop(1, TPS, lambda d: remote(
            send3.at[l], recv3.at[l, t], send_sem.at[l, 0], recv_sem.at[l, 0], (1, s, tp_peer(d))).start())

        @pl.when(l == 0)
        def _():
            own_loads[0].wait()

        @pl.when(l == 1)
        def _():
            wait_bytes(fgain.at[1], push_recv.at[1])
            wait_bytes(wgu.at[1], push_recv.at[3])

        wait_bytes(recv3.at[l, pl.ds(0, TPS - 1)], recv_sem.at[l, 0])
        after = (x_buf[...].astype(F32) + jnp.sum(recv3[l].astype(F32), axis=0)).astype(BF)
        a_buf[...] = after
        values = after.astype(F32)
        put_squares(values, l)
        loop(1, SHARDS, lambda d: send_squares(l, d))
        scaled = (values * fgain[l]).astype(BF)

        def go4(d):
            o = lax.rem(s + d, OWNERS)
            to = 4 * (o // 2) + 1 + o % 2
            both = jnp.dot(scaled, wgu[l, o], preferred_element_type=F32).astype(BF)

            @pl.when(to == s)
            def _():
                recv4[l, s] = both

            @pl.when(to != s)
            def _():
                send4[l, o] = both
                remote(send4.at[l, o], recv4.at[l, s], send_sem.at[l, 1], recv_sem.at[l, 1], (1, to, t)).start()

        loop(0, OWNERS, go4)
        factor = squares_factor(l)
        column = jnp.sum(jnp.where(diagonal, factor, 0.0), axis=1, keepdims=True)

        @pl.when(owns)
        def _():
            wait_bytes(recv4.at[l, pl.ds(0, SHARDS - 1)], recv_sem.at[l, 1])
            both = jnp.sum(recv4[l].astype(F32), axis=0) * column
            gate, up = both[:, :256], both[:, 256:]
            hidden = (gate / (1.0 + jnp.exp(-gate)) * up).astype(BF)
            send5[l] = hidden
            recv5[l, owner] = hidden
            loop(1, SHARDS, lambda d: remote(
                send5.at[l], recv5.at[l, owner], send_sem.at[l, 2], recv_sem.at[l, 2],
                (1, shard_peer(d), t)).start())

        @pl.when(l == 0)
        def _():
            scale_ref[1:2, :] = factor[:, :ROWS]
            own_loads[1].wait()

        @pl.when(l == 1)
        def _():
            end_scale[...] = factor
            remote(end_scale, end_scale, end_send.at[1], end_recv.at[1], mate).start()
            wait_bytes(wdn.at[1], push_recv.at[2])

        @pl.when(owns)
        def _():
            wait_bytes(recv5.at[l, pl.ds(0, OWNERS - 1)], recv_sem.at[l, 2])

        @pl.when(jnp.logical_not(owns))
        def _():
            wait_bytes(recv5.at[l], recv_sem.at[l, 2])

        hidden_all = jnp.concatenate([recv5[l, o] for o in range(OWNERS)], axis=1)
        partial = jnp.dot(hidden_all, wdn[l], preferred_element_type=F32).astype(BF)
        send6[l] = partial
        recv6[l, t] = partial
        loop(1, TPS, lambda d: remote(
            send6.at[l], recv6.at[l, t], send_sem.at[l, 3], recv_sem.at[l, 3], (1, s, tp_peer(d))).start())
        wait_bytes(recv6.at[l, pl.ds(0, TPS - 1)], recv_sem.at[l, 3])
        result = (a_buf[...].astype(F32) + jnp.sum(recv6[l].astype(F32), axis=0)).astype(BF)

        @pl.when(l == 0)
        def _():
            x_buf[...] = result
            out_ref[...] = result

        @pl.when(l == 1)
        def _():
            end_buf[...] = result
            remote(end_buf, end_buf, end_send.at[0], end_recv.at[0], mate).start()

    @pl.when(side == 1)
    def _():
        prepare(0)
        for load in first_loads + cache_loads:
            load.wait()
        pl.semaphore_wait(barrier, SHARDS - 1 + TPS - 1 + 1)

    def step(l):
        pl.when(side == l)(attention)

        @pl.when(side == 1)
        def _():
            layer(l)

    loop(0, 2, step)

    wait_bytes(ss_recv.at[2, pl.ds(0, SHARDS - 1)], ss_send_sem.at[2])
    wait_bytes(recv1.at[pl.ds(0, SHARDS - 1)], send1_sem)

    @pl.when(side == 0)
    def _():
        prepare(1)
        for push in pushes[1:]:
            push.start()
        wait_bytes(recv2.at[0], send2_sem)
        for push in pushes:
            push.wait_send()
        wait_bytes(end_scale, end_recv.at[1])
        scale_ref[1:2, :] = end_scale[:, :ROWS]
        wait_bytes(end_buf, end_recv.at[0])
        out_ref[...] = end_buf[...]

    @pl.when(side == 1)
    def _():
        wait_bytes(recv2.at[1, pl.ds(0, SHARDS - 1)], send2_sem)

        def sent(l):
            wait_bytes(ss_recv.at[l, pl.ds(0, SHARDS - 1)], ss_send_sem.at[l])
            wait_bytes(recv3.at[l, pl.ds(0, TPS - 1)], send_sem.at[l, 0])
            wait_bytes(recv6.at[l, pl.ds(0, TPS - 1)], send_sem.at[l, 3])

            @pl.when(owns)
            def _():
                wait_bytes(recv4.at[l, pl.ds(0, OWNERS - 1)], send_sem.at[l, 1])
                wait_bytes(recv4.at[l, pl.ds(0, SHARDS - 1), :, pl.ds(0, 256)], send_sem.at[l, 2])

            @pl.when(jnp.logical_not(owns))
            def _():
                wait_bytes(recv4.at[l, pl.ds(0, OWNERS)], send_sem.at[l, 1])

        loop(0, 2, sent)
        wait_bytes(end_buf, end_send.at[0])
        wait_bytes(end_scale, end_send.at[1])


def body(tokens, lengths, kv_cache, attn_gain, qkv_weight, out_weight, ffn_gain, gate_up, down_weight):
    freqs = (ROPE_BASE ** (-np.arange(HD // 2, dtype=np.float64) * 2.0 / HD)).astype(np.float32)
    freqs = jnp.asarray(np.concatenate([freqs, freqs])[None])
    vmem = pl.BlockSpec(memory_space=pltpu.VMEM)
    hbm = pl.BlockSpec(memory_space=pltpu.HBM)
    dma = pltpu.SemaphoreType.DMA
    out, scales = pl.pallas_call(
        kernel,
        out_shape=(jax.ShapeDtypeStruct((ROWS, 256), BF), jax.ShapeDtypeStruct((2, ROWS), F32)),
        in_specs=[hbm] * 10,
        out_specs=(vmem, vmem),
        scratch_shapes=[
            pltpu.SMEM((ROWS,), jnp.int32),
            pltpu.VMEM((1, 256), F32), pltpu.VMEM((2, 1, 256), F32), pltpu.VMEM((1, HD), F32),
            pltpu.VMEM((CTX, 2 * HD), BF), pltpu.VMEM((CTX, 2 * HD), BF),
            pltpu.VMEM((256, 768), BF), pltpu.VMEM((2, 512, 256), BF),
            pltpu.VMEM((TILES, 256, 2, HD), BF), pltpu.VMEM((2, OWNERS, 256, 512), BF),
            pltpu.VMEM((2, TILES * HD, 256), BF),
            pltpu.VMEM((ROWS, 256), BF), pltpu.VMEM((ROWS, 256), BF),
            pltpu.VMEM((3, 1, HD), F32), pltpu.VMEM((3, SHARDS, 1, HD), F32),
            pltpu.VMEM((16 * SHARDS, HD), F32), pltpu.VMEM((SHARDS, 16, HD), BF), pltpu.VMEM((SHARDS, 16, HD), BF),
            pltpu.VMEM((16, HD), BF), pltpu.VMEM((2, SHARDS, 16, HD), BF), pltpu.VMEM((16 * SHARDS, HD), F32),
            pltpu.VMEM((2, ROWS, 256), BF), pltpu.VMEM((2, TPS, ROWS, 256), BF),
            pltpu.VMEM((2, OWNERS, ROWS, 512), BF), pltpu.VMEM((2, SHARDS, ROWS, 512), BF),
            pltpu.VMEM((2, ROWS, 256), BF), pltpu.VMEM((2, OWNERS, ROWS, 256), BF),
            pltpu.VMEM((2, ROWS, 256), BF), pltpu.VMEM((2, TPS, ROWS, 256), BF),
            pltpu.VMEM((ROWS, 256), BF), pltpu.VMEM((1, HD), F32),
            dma((12,)), dma((TILES,)), dma((3,)), dma((3,)), dma, dma, dma, dma((2,)),
            dma((2, 4)), dma((2, 4)), dma((4,)), dma((4,)), dma((2,)), dma((2,)),
        ],
        compiler_params=pltpu.CompilerParams(
            collective_id=0, has_side_effects=True, vmem_limit_bytes=63 * 1024 * 1024),
        cost_estimate=pl.CostEstimate(flops=130_000_000, bytes_accessed=7_500_000, transcendentals=70_000),
    )(
        tokens, lengths, attn_gain, ffn_gain, freqs,
        kv_cache.reshape(2, CTX, 2 * HD), qkv_weight.reshape(256, 768), out_weight.reshape(512, 256),
        gate_up.reshape(256, 2, 1792), down_weight.reshape(1792, 256),
    )
    return (out[None], scales[None])


def solution(mesh):
    in_specs = (
        P(None, "shard"),
        P(),
        P("side", "shard", None, "tp", None),
        P("side", "shard"),
        P("side", "shard", "tp", None),
        P("side", "tp", None, "shard"),
        P("side", "shard"),
        P("side", "shard", None, "tp"),
        P("side", "tp", "shard"),
    )
    out_specs = (P("side", None, "shard"), P("side", None, None))
    return jax.shard_map(body, mesh=mesh, in_specs=in_specs, out_specs=out_specs, check_vma=False)
```

time: 95.2 us -> 77.6 us (0.82)
  the two profiles are of different devices: /device:TPU:6 before, /device:TPU:1 now
where the time goes in v2:
time: 77.6 us; the launch traced here: 77.3 us
  Pallas kernels  74.2 us (96%)
  local copies, waits for them, and re-layouts  2.54 us (3%)
    pallas_call x1, Pallas kernels, body(): pl.pallas_call(kernel, out_shape=(jax.ShapeDtypeStruct((ROWS, 256), BF),...  74.2 us
    unnamed x2, local copies, waits for them, and re-layouts  2.54 us

profile of v2, /device:TPU:1, one launch (start us, length us, event | category | flops | bytes accessed | tf_op | source)
XLA Modules:
  0.0 77.3 jit_solution(15873327734574551629)
XLA Ops:
  0.6 74.2 %shard_map.113 = (bf16[32,256]{1,0:T(8,128)(2,1)}, f32[2,32]{1,0:T(2,128)}) custom-call(bf16[32,256]{1,0:T(8,128)(2,1)} %tok_hbm.1, s32[32]{0:T(128)} %lens_hbm.1, f32[1,256]{1,0:T(1,128)} %again_hbm.1, f32[1,256]{1,0:T(1,128)} %fgain_hbm.1, f32[1,128]{1,0:T(1,128)} %constant.2.clone.freq_hbm, bf16[2,4096,256]{2,1,0:T(8,128)(2,1)} %bitcast.7, ...), custom_call_target="tpu_custom_call" | custom-call | flops 130000000 | bytes 7500000 | tf_op jit(solution)/shard_map/pallas_call | solution.py:416
  74.8 1.3 %copy.14 = bf16[1,32,256]{2,1,0:T(8,128)(2,1)} copy(bf16[1,32,256]{2,1,0:T(8,128)(2,1)} %bitcast.12) | data formatting | bytes 32768
  76.1 1.2 %copy.15 = f32[1,2,32]{2,1,0:T(2,128)} copy(f32[1,2,32]{2,1,0:T(2,128)} %bitcast.13) | data formatting | bytes 512

commit v3 on v2

--- a/solution.py
+++ b/solution.py
@@ -1,3 +1,5 @@
+import functools
+
 import jax
 import jax.numpy as jnp
 import numpy as np
@@ -16,6 +18,7 @@
 TILES = 14
 OWNERS = 7
 CTX = 4096
+CHUNK = 1024
 BF = jnp.bfloat16
 F32 = jnp.float32
 MESH = pl.DeviceIdType.MESH
@@ -38,12 +41,12 @@
     tok_hbm, lens_hbm, again_hbm, fgain_hbm, freq_hbm, cache_hbm, wqkv_hbm, wout_hbm, wgu_hbm, wdn_hbm,
     out_ref, scale_ref,
     lens, again, fgain, freq,
-    kbuf, vbuf, wqkv, wout, graw, wgu, wdn,
+    kbuf, vbuf, keys_t, wqkv, wout, graw, wgu, wdn,
     x_buf, a_buf,
     ss_send, ss_recv, stage, send1, recv1, send2, recv2, heads_f32,
-    send3, recv3, send4, recv4, send5, recv5, send6, recv6, end_buf, end_scale,
+    send3, recv3, send4, recv4, send5, recv5, send6, recv6, end_scale,
     load_sem, gu_sem, ss_send_sem, ss_recv_sem, send1_sem, recv1_sem, send2_sem, recv2_sem,
-    send_sem, recv_sem, push_send, push_recv, end_send, end_recv,
+    send_sem, recv_sem, recv6_sem, push_send, push_recv, end_send, end_recv,
 ):
     side = lax.axis_index("side")
     s = lax.axis_index("shard")
@@ -71,7 +74,7 @@
     @pl.when(side == 0)
     def _():
         loop(1, SHARDS, lambda d: greet((0, shard_peer(d), t)))
-        greet(mate)
+        loop(0, TPS, lambda d: greet((1, s, tp_peer(d))))
 
     @pl.when(side == 1)
     def _():
@@ -143,6 +146,19 @@
         wait_bytes(ss_recv.at[which, pl.ds(0, SHARDS - 1)], ss_recv_sem.at[which])
         return lax.rsqrt(jnp.sum(ss_recv[which], axis=0) / D + EPSILON)
 
+    def turn_keys():
+        for load in cache_loads:
+            load.wait()
+        eye = jnp.where(
+            lax.broadcasted_iota(jnp.int32, (256, 256), 0) == lax.broadcasted_iota(jnp.int32, (256, 256), 1),
+            1.0, 0.0).astype(BF)
+
+        def turn(c):
+            at = pl.ds(pl.multiple_of(512 * c, 512), 512)
+            keys_t[:, at] = nt_dot(eye, kbuf[at, :]).astype(BF)
+
+        loop(0, CTX // 512, turn)
+
     def attention():
         @pl.when(side == 0)
         def _():
@@ -174,6 +190,7 @@
             pushes[0].start()
             first_loads[3].wait()
             first_loads[4].wait()
+            turn_keys()
 
         lens_here = [lens[2 * s + i] for i in range(2)]
         upper_row = lax.broadcasted_iota(jnp.int32, (16, 1), 0) >= 8
@@ -199,19 +216,24 @@
         both = jnp.concatenate(
             [jnp.where(upper_row, 0.0, rotated), jnp.where(upper_row, rotated, 0.0)], axis=1).astype(BF)
 
-        @pl.when(side == 0)
-        def _():
-            for load in cache_loads:
-                load.wait()
-
-        scores = nt_dot(both, kbuf[...]) * HD ** (-0.5)
-        at = lax.broadcasted_iota(jnp.int32, (16, CTX), 1)
-        scores = jnp.where(at < position, scores, -1e30)
-        top = jnp.maximum(jnp.max(scores, axis=1, keepdims=True), own_score)
-        weights = jnp.exp(scores - top)
+        tops, sums, parts = [], [], []
+        for c in range(CTX // CHUNK):
+            scores = jnp.dot(both, keys_t[:, CHUNK * c:CHUNK * (c + 1)], preferred_element_type=F32) * HD ** (-0.5)
+            at = lax.broadcasted_iota(jnp.int32, (16, CHUNK), 1) + CHUNK * c
+            scores = jnp.where(at < position, scores, -1e30)
+            chunk_top = jnp.maximum(jnp.max(scores, axis=1, keepdims=True), own_score)
+            weights = jnp.exp(scores - chunk_top)
+            tops.append(chunk_top)
+            sums.append(jnp.sum(weights, axis=1, keepdims=True))
+            parts.append(jnp.dot(
+                weights.astype(BF), vbuf[CHUNK * c:CHUNK * (c + 1), :], preferred_element_type=F32))
+        top = functools.reduce(jnp.maximum, tops)
         own_weight = jnp.exp(own_score - top)
-        total = jnp.sum(weights, axis=1, keepdims=True) + own_weight
-        mixed_values = jnp.dot(weights.astype(BF), vbuf[...], preferred_element_type=F32)
+        total, mixed_values = own_weight, 0.0
+        for chunk_top, chunk_sum, part in zip(tops, sums, parts):
+            share = jnp.exp(chunk_top - top)
+            total = total + share * chunk_sum
+            mixed_values = mixed_values + share * part
         mixed_values = jnp.concatenate([mixed_values[:8, :HD], mixed_values[8:, HD:]], axis=0)
         mixed_values = mixed_values + own_weight.astype(BF).astype(F32) * new_value
         heads = (mixed_values / total).astype(BF)
@@ -284,18 +306,19 @@
         loop(1, SHARDS, lambda d: send_squares(l, d))
         scaled = (values * fgain[l]).astype(BF)
 
+        for o in range(OWNERS):
+            send4[l, o] = jnp.dot(scaled, wgu[l, o], preferred_element_type=F32).astype(BF)
+
+        @pl.when(owns)
+        def _():
+            recv4[l, s] = send4[l, jnp.where(owns, owner, 0)]
+
         def go4(d):
             o = lax.rem(s + d, OWNERS)
             to = 4 * (o // 2) + 1 + o % 2
-            both = jnp.dot(scaled, wgu[l, o], preferred_element_type=F32).astype(BF)
-
-            @pl.when(to == s)
-            def _():
-                recv4[l, s] = both
 
             @pl.when(to != s)
             def _():
-                send4[l, o] = both
                 remote(send4.at[l, o], recv4.at[l, s], send_sem.at[l, 1], recv_sem.at[l, 1], (1, to, t)).start()
 
         loop(0, OWNERS, go4)
@@ -323,6 +346,7 @@
         def _():
             end_scale[...] = factor
             remote(end_scale, end_scale, end_send.at[1], end_recv.at[1], mate).start()
+            remote(a_buf, a_buf, end_send.at[0], end_recv.at[0], mate).start()
             wait_bytes(wdn.at[1], push_recv.at[2])
 
         @pl.when(owns)
@@ -336,28 +360,29 @@
         hidden_all = jnp.concatenate([recv5[l, o] for o in range(OWNERS)], axis=1)
         partial = jnp.dot(hidden_all, wdn[l], preferred_element_type=F32).astype(BF)
         send6[l] = partial
-        recv6[l, t] = partial
-        loop(1, TPS, lambda d: remote(
-            send6.at[l], recv6.at[l, t], send_sem.at[l, 3], recv_sem.at[l, 3], (1, s, tp_peer(d))).start())
-        wait_bytes(recv6.at[l, pl.ds(0, TPS - 1)], recv_sem.at[l, 3])
-        result = (a_buf[...].astype(F32) + jnp.sum(recv6[l].astype(F32), axis=0)).astype(BF)
 
         @pl.when(l == 0)
         def _():
+            recv6[t] = partial
+            loop(1, TPS, lambda d: remote(
+                send6.at[l], recv6.at[t], send_sem.at[l, 3], recv6_sem, (1, s, tp_peer(d))).start())
+            wait_bytes(recv6.at[pl.ds(0, TPS - 1)], recv6_sem)
+            result = (a_buf[...].astype(F32) + jnp.sum(recv6[...].astype(F32), axis=0)).astype(BF)
             x_buf[...] = result
             out_ref[...] = result
 
         @pl.when(l == 1)
         def _():
-            end_buf[...] = result
-            remote(end_buf, end_buf, end_send.at[0], end_recv.at[0], mate).start()
+            loop(0, TPS, lambda d: remote(
+                send6.at[l], recv6.at[t], send_sem.at[l, 3], recv6_sem, (0, s, tp_peer(d))).start())
 
     @pl.when(side == 1)
     def _():
         prepare(0)
-        for load in first_loads + cache_loads:
+        for load in first_loads:
             load.wait()
-        pl.semaphore_wait(barrier, SHARDS - 1 + TPS - 1 + 1)
+        turn_keys()
+        pl.semaphore_wait(barrier, SHARDS - 1 + TPS - 1 + TPS)
 
     def step(l):
         pl.when(side == l)(attention)
@@ -381,8 +406,9 @@
             push.wait_send()
         wait_bytes(end_scale, end_recv.at[1])
         scale_ref[1:2, :] = end_scale[:, :ROWS]
-        wait_bytes(end_buf, end_recv.at[0])
-        out_ref[...] = end_buf[...]
+        wait_bytes(a_buf, end_recv.at[0])
+        wait_bytes(recv6, recv6_sem)
+        out_ref[...] = (a_buf[...].astype(F32) + jnp.sum(recv6[...].astype(F32), axis=0)).astype(BF)
 
     @pl.when(side == 1)
     def _():
@@ -391,7 +417,6 @@
         def sent(l):
             wait_bytes(ss_recv.at[l, pl.ds(0, SHARDS - 1)], ss_send_sem.at[l])
             wait_bytes(recv3.at[l, pl.ds(0, TPS - 1)], send_sem.at[l, 0])
-            wait_bytes(recv6.at[l, pl.ds(0, TPS - 1)], send_sem.at[l, 3])
 
             @pl.when(owns)
             def _():
@@ -403,7 +428,9 @@
                 wait_bytes(recv4.at[l, pl.ds(0, OWNERS)], send_sem.at[l, 1])
 
         loop(0, 2, sent)
-        wait_bytes(end_buf, end_send.at[0])
+        wait_bytes(recv6.at[pl.ds(0, TPS - 1)], send_sem.at[0, 3])
+        wait_bytes(recv6, send_sem.at[1, 3])
+        wait_bytes(a_buf, end_send.at[0])
         wait_bytes(end_scale, end_send.at[1])
 
 
@@ -415,13 +442,13 @@
     dma = pltpu.SemaphoreType.DMA
     out, scales = pl.pallas_call(
         kernel,
-        out_shape=(jax.ShapeDtypeStruct((ROWS, 256), BF), jax.ShapeDtypeStruct((2, ROWS), F32)),
+        out_shape=(pltpu.VMEM((ROWS, 256), BF), pltpu.VMEM((2, ROWS), F32)),
         in_specs=[hbm] * 10,
         out_specs=(vmem, vmem),
         scratch_shapes=[
             pltpu.SMEM((ROWS,), jnp.int32),
             pltpu.VMEM((1, 256), F32), pltpu.VMEM((2, 1, 256), F32), pltpu.VMEM((1, HD), F32),
-            pltpu.VMEM((CTX, 2 * HD), BF), pltpu.VMEM((CTX, 2 * HD), BF),
+            pltpu.VMEM((CTX, 2 * HD), BF), pltpu.VMEM((CTX, 2 * HD), BF), pltpu.VMEM((2 * HD, CTX), BF),
             pltpu.VMEM((256, 768), BF), pltpu.VMEM((2, 512, 256), BF),
             pltpu.VMEM((TILES, 256, 2, HD), BF), pltpu.VMEM((2, OWNERS, 256, 512), BF),
             pltpu.VMEM((2, TILES * HD, 256), BF),
@@ -432,19 +459,19 @@
             pltpu.VMEM((2, ROWS, 256), BF), pltpu.VMEM((2, TPS, ROWS, 256), BF),
             pltpu.VMEM((2, OWNERS, ROWS, 512), BF), pltpu.VMEM((2, SHARDS, ROWS, 512), BF),
             pltpu.VMEM((2, ROWS, 256), BF), pltpu.VMEM((2, OWNERS, ROWS, 256), BF),
-            pltpu.VMEM((2, ROWS, 256), BF), pltpu.VMEM((2, TPS, ROWS, 256), BF),
-            pltpu.VMEM((ROWS, 256), BF), pltpu.VMEM((1, HD), F32),
+            pltpu.VMEM((2, ROWS, 256), BF), pltpu.VMEM((TPS, ROWS, 256), BF),
+            pltpu.VMEM((1, HD), F32),
             dma((12,)), dma((TILES,)), dma((3,)), dma((3,)), dma, dma, dma, dma((2,)),
-            dma((2, 4)), dma((2, 4)), dma((4,)), dma((4,)), dma((2,)), dma((2,)),
+            dma((2, 4)), dma((2, 3)), dma, dma((4,)), dma((4,)), dma((2,)), dma((2,)),
         ],
         compiler_params=pltpu.CompilerParams(
             collective_id=0, has_side_effects=True, vmem_limit_bytes=63 * 1024 * 1024),
         cost_estimate=pl.CostEstimate(flops=130_000_000, bytes_accessed=7_500_000, transcendentals=70_000),
-    )(
+    )(*(pltpu.with_memory_space_constraint(x, pltpu.HBM) for x in (
         tokens, lengths, attn_gain, ffn_gain, freqs,
         kv_cache.reshape(2, CTX, 2 * HD), qkv_weight.reshape(256, 768), out_weight.reshape(512, 256),
         gate_up.reshape(256, 2, 1792), down_weight.reshape(1792, 256),
-    )
+    )))
     return (out[None], scales[None])
 
 

time: 77.6 us -> 73.5 us (0.947)
  the two profiles are of different devices: /device:TPU:1 before, /device:TPU:6 now
where the time goes in v3:
time: 73.5 us; the launch traced here: 73.3 us
  Pallas kernels  71.5 us (97%)
  local copies, waits for them, and re-layouts  1.17 us (2%)
    pallas_call x1, Pallas kernels, body(): pl.pallas_call(kernel, out_shape=(pltpu.VMEM((ROWS, 256), BF), pltpu.VMEM...  71.5 us

profile of v3, /device:TPU:6, one launch (start us, length us, event | category | flops | bytes accessed | tf_op | source)
XLA Modules:
  0.0 73.3 jit_solution(15602368517006524489)
XLA Ops:
  0.6 71.5 %shard_map.113 = (bf16[32,256]{1,0:T(8,128)(2,1)S(1)}, f32[2,32]{1,0:T(2,128)S(1)}) custom-call(bf16[32,256]{1,0:T(8,128)(2,1)} %tok_hbm.1, s32[32]{0:T(128)} %lens_hbm.1, f32[1,256]{1,0:T(1,128)} %again_hbm.1, f32[1,256]{1,0:T(1,128)} %fgain_hbm.1, f32[1,128]{1,0:T(1,128)} %constant.2.clone.freq_hbm, bf16[2,4096,256]{2,1,0:T(8,128)(2,1)} %bitcast.9, ...), custom_call_target="tpu_custom_call" | custom-call | flops 130000000 | bytes 7500000 | tf_op jit(solution)/shard_map/pallas_call | solution.py:443
  72.2 0.6 copy.14
  72.8 0.6 copy.15

commit v4 on v3

--- a/solution.py
+++ b/solution.py
@@ -46,18 +46,28 @@
     ss_send, ss_recv, stage, send1, recv1, send2, recv2, heads_f32,
     send3, recv3, send4, recv4, send5, recv5, send6, recv6, end_scale,
     load_sem, gu_sem, ss_send_sem, ss_recv_sem, send1_sem, recv1_sem, send2_sem, recv2_sem,
-    send_sem, recv_sem, recv6_sem, push_send, push_recv, end_send, end_recv,
+    send_sem, recv_sem, recv6_sem, push_send, push_recv, end_send, end_recv, ready,
 ):
     side = lax.axis_index("side")
     s = lax.axis_index("shard")
     t = lax.axis_index("tp")
     mate = (1 - side, s, t)
+    y, x, half = s // 4, t % 4, t // 4
+    z = 4 * half + s % 4
+    across = (1, s, 4 * (1 - half) + x)
 
     def shard_peer(d):
         return lax.rem(s + d, SHARDS)
 
     def tp_peer(d):
         return lax.rem(t + d, TPS)
+
+    def x_peer(d):
+        return 4 * half + lax.rem(x + d, 4)
+
+    def plane_peer(at_side, dy, dz):
+        to_z = lax.rem(z + dz, 8)
+        return (at_side, 4 * lax.rem(y + dy, 4) + lax.rem(to_z, 4), 4 * (to_z // 4) + x)
 
     barrier = pltpu.get_barrier_semaphore()
 
@@ -71,16 +81,32 @@
 
         lax.fori_loop(start, stop, go, 0)
 
+    def plane(step):
+        loop(0, 32, lambda e: step(lax.rem(e // 8 + 2, 4), lax.rem(e + 4, 8)))
+
+    def shard_peers(step):
+        loop(8, SHARDS, step)
+        loop(1, 8, step)
+
+    def greet_side_1():
+        def in_plane(dy, dz):
+            @pl.when((side == 0) | (dy != 0) | (dz != 0))
+            def _():
+                greet(plane_peer(1, dy, dz))
+
+        plane(in_plane)
+
+        def other_x(d):
+            greet((1, s, x_peer(d)))
+            greet((1, s, lax.rem(4 + x_peer(d), TPS)))
+
+        loop(1, 4, other_x)
+
     @pl.when(side == 0)
     def _():
-        loop(1, SHARDS, lambda d: greet((0, shard_peer(d), t)))
-        loop(0, TPS, lambda d: greet((1, s, tp_peer(d))))
-
-    @pl.when(side == 1)
-    def _():
-        loop(0, SHARDS, lambda d: greet((0, shard_peer(d), t)))
-        loop(1, SHARDS, lambda d: greet((1, shard_peer(d), t)))
-        loop(1, TPS, lambda d: greet((1, s, tp_peer(d))))
+        shard_peers(lambda d: greet((0, shard_peer(d), t)))
+
+    greet_side_1()
 
     first_loads = [
         pltpu.make_async_copy(tok_hbm, x_buf, load_sem.at[0]),
@@ -98,7 +124,7 @@
     own_loads = [
         pltpu.make_async_copy(fgain_hbm, fgain.at[0], load_sem.at[9]),
         pltpu.make_async_copy(wdn_hbm, wdn.at[0], load_sem.at[10]),
-        pltpu.make_async_copy(wout_hbm, wout.at[1], load_sem.at[11]),
+        pltpu.make_async_copy(wout_hbm, wout.at[1, half], load_sem.at[11]),
     ]
     gu_loads = [
         pltpu.make_async_copy(wgu_hbm.at[:, :, pl.ds(HD * j, HD)], graw.at[j], gu_sem.at[j]) for j in range(TILES)
@@ -122,11 +148,14 @@
             load.start()
 
     pushes = [
-        remote(wout_hbm, wout.at[0], push_send.at[0], push_recv.at[0], mate),
+        remote(wout_hbm, wout.at[0, half], push_send.at[0], push_recv.at[0], mate),
+        remote(wout_hbm, wout.at[0, half], push_send.at[4], push_recv.at[4], across),
         remote(fgain_hbm, fgain.at[1], push_send.at[1], push_recv.at[1], mate),
         remote(wdn_hbm, wdn.at[1], push_send.at[2], push_recv.at[2], mate),
         remote(wgu.at[1], wgu.at[1], push_send.at[3], push_recv.at[3], mate),
     ]
+
+    cross_push = remote(wout_hbm, wout.at[1, half], push_send.at[5], push_recv.at[5], across)
 
     stage[...] = jnp.zeros_like(stage)
     diagonal = lax.broadcasted_iota(jnp.int32, (ROWS, HD), 0) == lax.broadcasted_iota(jnp.int32, (ROWS, HD), 1)
@@ -176,21 +205,23 @@
 
         @pl.when(side == 0)
         def _():
-            pl.semaphore_wait(barrier, 2 * SHARDS - 1)
+            pl.semaphore_wait(barrier, SHARDS - 1)
 
         def go1(d):
             to = shard_peer(d)
             send_squares(2, d)
             remote(send1.at[to], recv1.at[s], send1_sem, recv1_sem, (side, to, t)).start()
 
-        loop(1, SHARDS, go1)
+        shard_peers(go1)
 
         @pl.when(side == 0)
         def _():
-            pushes[0].start()
             first_loads[3].wait()
             first_loads[4].wait()
             turn_keys()
+            pl.semaphore_wait(ready, 32)
+            pushes[0].start()
+            pushes[1].start()
 
         lens_here = [lens[2 * s + i] for i in range(2)]
         upper_row = lax.broadcasted_iota(jnp.int32, (16, 1), 0) >= 8
@@ -236,19 +267,21 @@
             mixed_values = mixed_values + share * part
         mixed_values = jnp.concatenate([mixed_values[:8, :HD], mixed_values[8:, HD:]], axis=0)
         mixed_values = mixed_values + own_weight.astype(BF).astype(F32) * new_value
-        heads = (mixed_values / total).astype(BF)
+        heads = mixed_values / total
+        heads = jnp.concatenate([heads[0:4], heads[8:12]], axis=0).astype(BF)
         send2[...] = heads
 
         @pl.when(side == 1)
         def _():
-            recv2[1, s] = heads
-
-        @pl.when(side == 0)
-        def _():
-            remote(send2, recv2.at[side, s], send2_sem, recv2_sem.at[side], mate).start()
-
-        loop(1, SHARDS, lambda d: remote(
-            send2, recv2.at[side, s], send2_sem, recv2_sem.at[side], (1, shard_peer(d), t)).start())
+            recv2[1, SHARDS * half + s] = heads
+
+        def go2(dy, dz):
+            @pl.when((side == 0) | (dy != 0) | (dz != 0))
+            def _():
+                remote(send2, recv2.at[side, SHARDS * half + s], send2_sem, recv2_sem.at[side],
+                       plane_peer(1, dy, dz)).start()
+
+        plane(go2)
 
     def prepare(slot):
         for load in gu_loads:
@@ -272,25 +305,28 @@
     def layer(l):
         @pl.when(l == 0)
         def _():
-            wait_bytes(wout.at[0], push_recv.at[0])
+            wait_bytes(wout.at[0, 0], push_recv.at[0])
+            wait_bytes(wout.at[0, 0], push_recv.at[4])
             wait_bytes(recv2.at[0], recv2_sem.at[0])
 
         @pl.when(l == 1)
         def _():
             own_loads[2].wait()
-            wait_bytes(recv2.at[1, pl.ds(0, SHARDS - 1)], recv2_sem.at[1])
-
-        heads_f32[...] = recv2[l].astype(F32).reshape(16 * SHARDS, HD)
+            wait_bytes(wout.at[1, 0], push_recv.at[5])
+            wait_bytes(recv2.at[1, pl.ds(0, 31)], recv2_sem.at[1])
+
+        heads_f32[...] = recv2[l].astype(F32).reshape(256, HD)
         gathered = jnp.concatenate(
-            [heads_f32[pl.ds(g, ROWS, stride=8), :] for g in range(4)], axis=1).astype(BF)
-        projected = jnp.dot(gathered, wout[l], preferred_element_type=F32).astype(BF)
+            [heads_f32[pl.ds(128 * h + g, ROWS, stride=4), :] for h in range(2) for g in range(4)], axis=1).astype(BF)
+        projected = jnp.dot(gathered, wout[l].reshape(1024, 256), preferred_element_type=F32).astype(BF)
         send3[l] = projected
-        recv3[l, t] = projected
-        loop(1, TPS, lambda d: remote(
-            send3.at[l], recv3.at[l, t], send_sem.at[l, 0], recv_sem.at[l, 0], (1, s, tp_peer(d))).start())
+        recv3[l, x] = projected
+        loop(1, 4, lambda d: remote(
+            send3.at[l], recv3.at[l, x], send_sem.at[l, 0], recv_sem.at[l, 0], (1, s, x_peer(d))).start())
 
         @pl.when(l == 0)
         def _():
+            cross_push.start()
             own_loads[0].wait()
 
         @pl.when(l == 1)
@@ -298,30 +334,30 @@
             wait_bytes(fgain.at[1], push_recv.at[1])
             wait_bytes(wgu.at[1], push_recv.at[3])
 
-        wait_bytes(recv3.at[l, pl.ds(0, TPS - 1)], recv_sem.at[l, 0])
+        wait_bytes(recv3.at[l, pl.ds(0, 3)], recv_sem.at[l, 0])
         after = (x_buf[...].astype(F32) + jnp.sum(recv3[l].astype(F32), axis=0)).astype(BF)
         a_buf[...] = after
         values = after.astype(F32)
         put_squares(values, l)
-        loop(1, SHARDS, lambda d: send_squares(l, d))
+        shard_peers(lambda d: send_squares(l, d))
         scaled = (values * fgain[l]).astype(BF)
 
-        for o in range(OWNERS):
-            send4[l, o] = jnp.dot(scaled, wgu[l, o], preferred_element_type=F32).astype(BF)
-
-        @pl.when(owns)
-        def _():
-            recv4[l, s] = send4[l, jnp.where(owns, owner, 0)]
-
-        def go4(d):
-            o = lax.rem(s + d, OWNERS)
-            to = 4 * (o // 2) + 1 + o % 2
-
-            @pl.when(to != s)
-            def _():
-                remote(send4.at[l, o], recv4.at[l, s], send_sem.at[l, 1], recv_sem.at[l, 1], (1, to, t)).start()
-
-        loop(0, OWNERS, go4)
+
+        for d in range(OWNERS):
+            o = lax.rem(jnp.where(owns, owner + 1, s) + d, OWNERS)
+            both = jnp.dot(scaled, wgu[l, o], preferred_element_type=F32).astype(BF)
+            send4[l, o] = both
+            send = remote(send4.at[l, o], recv4.at[l, s], send_sem.at[l, 1], recv_sem.at[l, 1],
+                          (1, 4 * (o // 2) + 1 + o % 2, t))
+            if d < OWNERS - 1:
+                send.start()
+            else:
+                pl.when(jnp.logical_not(owns))(send.start)
+
+                @pl.when(owns)
+                def _():
+                    recv4[l, s] = both
+
         factor = squares_factor(l)
         column = jnp.sum(jnp.where(diagonal, factor, 0.0), axis=1, keepdims=True)
 
@@ -333,7 +369,7 @@
             hidden = (gate / (1.0 + jnp.exp(-gate)) * up).astype(BF)
             send5[l] = hidden
             recv5[l, owner] = hidden
-            loop(1, SHARDS, lambda d: remote(
+            shard_peers(lambda d: remote(
                 send5.at[l], recv5.at[l, owner], send_sem.at[l, 2], recv_sem.at[l, 2],
                 (1, shard_peer(d), t)).start())
 
@@ -378,11 +414,13 @@
 
     @pl.when(side == 1)
     def _():
+        pl.semaphore_wait(barrier, 38 + 37)
+        plane(lambda dy, dz: pl.semaphore_signal(
+            ready, inc=1, device_id=plane_peer(0, dy, dz), device_id_type=MESH))
         prepare(0)
         for load in first_loads:
             load.wait()
         turn_keys()
-        pl.semaphore_wait(barrier, SHARDS - 1 + TPS - 1 + TPS)
 
     def step(l):
         pl.when(side == l)(attention)
@@ -399,7 +437,7 @@
     @pl.when(side == 0)
     def _():
         prepare(1)
-        for push in pushes[1:]:
+        for push in pushes[2:]:
             push.start()
         wait_bytes(recv2.at[0], send2_sem)
         for push in pushes:
@@ -412,11 +450,12 @@
 
     @pl.when(side == 1)
     def _():
-        wait_bytes(recv2.at[1, pl.ds(0, SHARDS - 1)], send2_sem)
+        wait_bytes(recv2.at[1, pl.ds(0, 31)], send2_sem)
+        cross_push.wait_send()
 
         def sent(l):
             wait_bytes(ss_recv.at[l, pl.ds(0, SHARDS - 1)], ss_send_sem.at[l])
-            wait_bytes(recv3.at[l, pl.ds(0, TPS - 1)], send_sem.at[l, 0])
+            wait_bytes(recv3.at[l, pl.ds(0, 3)], send_sem.at[l, 0])
 
             @pl.when(owns)
             def _():
@@ -449,20 +488,21 @@
             pltpu.SMEM((ROWS,), jnp.int32),
             pltpu.VMEM((1, 256), F32), pltpu.VMEM((2, 1, 256), F32), pltpu.VMEM((1, HD), F32),
             pltpu.VMEM((CTX, 2 * HD), BF), pltpu.VMEM((CTX, 2 * HD), BF), pltpu.VMEM((2 * HD, CTX), BF),
-            pltpu.VMEM((256, 768), BF), pltpu.VMEM((2, 512, 256), BF),
+            pltpu.VMEM((256, 768), BF), pltpu.VMEM((2, 2, 512, 256), BF),
             pltpu.VMEM((TILES, 256, 2, HD), BF), pltpu.VMEM((2, OWNERS, 256, 512), BF),
             pltpu.VMEM((2, TILES * HD, 256), BF),
             pltpu.VMEM((ROWS, 256), BF), pltpu.VMEM((ROWS, 256), BF),
             pltpu.VMEM((3, 1, HD), F32), pltpu.VMEM((3, SHARDS, 1, HD), F32),
             pltpu.VMEM((16 * SHARDS, HD), F32), pltpu.VMEM((SHARDS, 16, HD), BF), pltpu.VMEM((SHARDS, 16, HD), BF),
-            pltpu.VMEM((16, HD), BF), pltpu.VMEM((2, SHARDS, 16, HD), BF), pltpu.VMEM((16 * SHARDS, HD), F32),
-            pltpu.VMEM((2, ROWS, 256), BF), pltpu.VMEM((2, TPS, ROWS, 256), BF),
+            pltpu.VMEM((8, HD), BF), pltpu.VMEM((2, 2 * SHARDS, 8, HD), BF), pltpu.VMEM((256, HD), F32),
+            pltpu.VMEM((2, ROWS, 256), BF), pltpu.VMEM((2, 4, ROWS, 256), BF),
             pltpu.VMEM((2, OWNERS, ROWS, 512), BF), pltpu.VMEM((2, SHARDS, ROWS, 512), BF),
             pltpu.VMEM((2, ROWS, 256), BF), pltpu.VMEM((2, OWNERS, ROWS, 256), BF),
             pltpu.VMEM((2, ROWS, 256), BF), pltpu.VMEM((TPS, ROWS, 256), BF),
             pltpu.VMEM((1, HD), F32),
             dma((12,)), dma((TILES,)), dma((3,)), dma((3,)), dma, dma, dma, dma((2,)),
-            dma((2, 4)), dma((2, 3)), dma, dma((4,)), dma((4,)), dma((2,)), dma((2,)),
+            dma((2, 4)), dma((2, 3)), dma, dma((6,)), dma((6,)), dma((2,)), dma((2,)),
+            pltpu.SemaphoreType.REGULAR,
         ],
         compiler_params=pltpu.CompilerParams(
             collective_id=0, has_side_effects=True, vmem_limit_bytes=63 * 1024 * 1024),

time: 73.5 us -> 81.8 us (1.11)
  Pallas kernels: 71.5 us -> 79.8 us
    pallas_call x1, Pallas kernels: 71.5 us -> 79.8 us  [body(): pl.pallas_call(kernel, out_shape=(pltpu.VMEM((ROWS, 256), BF), pltpu.VMEM...]
where the time goes in v4:
time: 81.8 us; the launch traced here: 81.6 us
  Pallas kernels  79.8 us (98%)
  local copies, waits for them, and re-layouts  1.17 us (1%)
    pallas_call x1, Pallas kernels, body(): pl.pallas_call(kernel, out_shape=(pltpu.VMEM((ROWS, 256), BF), pltpu.VMEM...  79.8 us

profile of v4, /device:TPU:6, one launch (start us, length us, event | category | flops | bytes accessed | tf_op | source)
XLA Modules:
  0.0 81.6 jit_solution(4840581913841545700)
XLA Ops:
  0.6 79.8 %shard_map.113 = (bf16[32,256]{1,0:T(8,128)(2,1)S(1)}, f32[2,32]{1,0:T(2,128)S(1)}) custom-call(bf16[32,256]{1,0:T(8,128)(2,1)} %tok_hbm.1, s32[32]{0:T(128)} %lens_hbm.1, f32[1,256]{1,0:T(1,128)} %again_hbm.1, f32[1,256]{1,0:T(1,128)} %fgain_hbm.1, f32[1,128]{1,0:T(1,128)} %constant.2.clone.freq_hbm, bf16[2,4096,256]{2,1,0:T(8,128)(2,1)} %bitcast.9, ...), custom_call_target="tpu_custom_call" | custom-call | flops 130000000 | bytes 7500000 | tf_op jit(solution)/shard_map/pallas_call | solution.py:482
  80.5 0.6 copy.14
  81.1 0.6 copy.15

commit v5 on v3

--- a/solution.py
+++ b/solution.py
@@ -98,13 +98,14 @@
     own_loads = [
         pltpu.make_async_copy(fgain_hbm, fgain.at[0], load_sem.at[9]),
         pltpu.make_async_copy(wdn_hbm, wdn.at[0], load_sem.at[10]),
-        pltpu.make_async_copy(wout_hbm, wout.at[1], load_sem.at[11]),
+        pltpu.make_async_copy(wout_hbm, wout.at[side], load_sem.at[11]),
     ]
     gu_loads = [
         pltpu.make_async_copy(wgu_hbm.at[:, :, pl.ds(HD * j, HD)], graw.at[j], gu_sem.at[j]) for j in range(TILES)
     ]
     for load in first_loads:
         load.start()
+    own_loads[2].start()
 
     @pl.when(side == 0)
     def _():
@@ -116,19 +117,18 @@
 
     @pl.when(side == 1)
     def _():
-        for load in own_loads:
+        for load in own_loads[:2]:
             load.start()
         for load in cache_loads:
             load.start()
 
     pushes = [
-        remote(wout_hbm, wout.at[0], push_send.at[0], push_recv.at[0], mate),
+        remote(wout.at[0], wout.at[0], push_send.at[0], push_recv.at[0], mate),
         remote(fgain_hbm, fgain.at[1], push_send.at[1], push_recv.at[1], mate),
         remote(wdn_hbm, wdn.at[1], push_send.at[2], push_recv.at[2], mate),
         remote(wgu.at[1], wgu.at[1], push_send.at[3], push_recv.at[3], mate),
     ]
 
-    stage[...] = jnp.zeros_like(stage)
     diagonal = lax.broadcasted_iota(jnp.int32, (ROWS, HD), 0) == lax.broadcasted_iota(jnp.int32, (ROWS, HD), 1)
     lane = lax.broadcasted_iota(jnp.int32, (1, HD), 1)
 
@@ -171,6 +171,10 @@
         mixed = jnp.dot((values * again[...]).astype(BF), wqkv[...], preferred_element_type=F32)
         for part in range(6):
             stage[pl.ds(part, ROWS, stride=8), :] = mixed[:, HD * part:HD * (part + 1)]
+        column = jnp.broadcast_to(jnp.sum(values * values, axis=1, keepdims=True), (ROWS, HD))
+        rounded = column.astype(BF).astype(F32)
+        stage[pl.ds(6, ROWS, stride=8), :] = rounded
+        stage[pl.ds(7, ROWS, stride=8), :] = column - rounded
         send1[...] = stage[...].astype(BF).reshape(SHARDS, 16, HD)
         recv1[s] = send1[s]
 
@@ -180,13 +184,14 @@
 
         def go1(d):
             to = shard_peer(d)
-            send_squares(2, d)
             remote(send1.at[to], recv1.at[s], send1_sem, recv1_sem, (side, to, t)).start()
 
         loop(1, SHARDS, go1)
+        loop(1, SHARDS, lambda d: send_squares(2, d))
 
         @pl.when(side == 0)
         def _():
+            own_loads[2].wait()
             pushes[0].start()
             first_loads[3].wait()
             first_loads[4].wait()
@@ -199,12 +204,11 @@
         cosine = jnp.cos(angle)
         sine = jnp.where(lane < HD // 2, -jnp.sin(angle), jnp.sin(angle))
 
-        factor = squares_factor(2)
-        scale_ref[0:1, :] = factor[:, :ROWS]
-        own_factor = jnp.sum(
-            jnp.where(lane == jnp.where(upper_row, 2 * s + 1, 2 * s), factor, 0.0), axis=1, keepdims=True)
         wait_bytes(recv1.at[pl.ds(0, SHARDS - 1)], recv1_sem)
-        own = jnp.sum(recv1[...].astype(F32), axis=0) * own_factor
+        own = jnp.sum(recv1[...].astype(F32), axis=0)
+        squares = jnp.concatenate(
+            [jnp.broadcast_to(own[8 * i + 6:8 * i + 7] + own[8 * i + 7:8 * i + 8], (8, HD)) for i in range(2)], axis=0)
+        own = own * lax.rsqrt(squares / D + EPSILON)
         rotated = own * cosine + pltpu.roll(own, HD // 2, 1) * sine
         rotated = rotated.astype(BF).astype(F32)
         own_values = own.astype(BF).astype(F32)
@@ -236,7 +240,8 @@
             mixed_values = mixed_values + share * part
         mixed_values = jnp.concatenate([mixed_values[:8, :HD], mixed_values[8:, HD:]], axis=0)
         mixed_values = mixed_values + own_weight.astype(BF).astype(F32) * new_value
-        heads = (mixed_values / total).astype(BF)
+        heads = mixed_values / total
+        heads = jnp.concatenate([heads[0:4], heads[8:12]], axis=0).astype(BF)
         send2[...] = heads
 
         @pl.when(side == 1)
@@ -249,6 +254,7 @@
 
         loop(1, SHARDS, lambda d: remote(
             send2, recv2.at[side, s], send2_sem, recv2_sem.at[side], (1, shard_peer(d), t)).start())
+        scale_ref[0:1, :] = squares_factor(2)[:, :ROWS]
 
     def prepare(slot):
         for load in gu_loads:
@@ -259,10 +265,11 @@
         pick = jnp.where(in_row == wanted, 1.0, 0.0).astype(BF)
 
         def one(o):
-            for half in range(2):
-                apart = jnp.dot(pick, graw[2 * o + half].reshape(512, HD), preferred_element_type=F32).astype(BF)
-                wgu[slot, o, :, HD * half:HD * (half + 1)] = apart[:256]
-                wgu[slot, o, :, 256 + HD * half:256 + HD * (half + 1)] = apart[256:]
+            raw = jnp.concatenate([graw[2 * o].reshape(512, HD), graw[2 * o + 1].reshape(512, HD)], axis=1)
+            apart = jnp.dot(pick, raw, preferred_element_type=F32).astype(BF)
+            for part in range(4):
+                wgu[slot, o, :, HD * part:HD * (part + 1)] = apart[
+                    256 * (part % 2):256 * (part % 2 + 1), HD * (part // 2):HD * (part // 2 + 1)]
 
         loop(0, OWNERS, one)
 
@@ -280,9 +287,9 @@
             own_loads[2].wait()
             wait_bytes(recv2.at[1, pl.ds(0, SHARDS - 1)], recv2_sem.at[1])
 
-        heads_f32[...] = recv2[l].astype(F32).reshape(16 * SHARDS, HD)
+        heads_f32[...] = recv2[l].astype(F32).reshape(8 * SHARDS, HD)
         gathered = jnp.concatenate(
-            [heads_f32[pl.ds(g, ROWS, stride=8), :] for g in range(4)], axis=1).astype(BF)
+            [heads_f32[pl.ds(g, ROWS, stride=4), :] for g in range(4)], axis=1).astype(BF)
         projected = jnp.dot(gathered, wout[l], preferred_element_type=F32).astype(BF)
         send3[l] = projected
         recv3[l, t] = projected
@@ -303,39 +310,43 @@
         a_buf[...] = after
         values = after.astype(F32)
         put_squares(values, l)
-        loop(1, SHARDS, lambda d: send_squares(l, d))
         scaled = (values * fgain[l]).astype(BF)
 
-        for o in range(OWNERS):
-            send4[l, o] = jnp.dot(scaled, wgu[l, o], preferred_element_type=F32).astype(BF)
-
-        @pl.when(owns)
-        def _():
-            recv4[l, s] = send4[l, jnp.where(owns, owner, 0)]
-
-        def go4(d):
-            o = lax.rem(s + d, OWNERS)
-            to = 4 * (o // 2) + 1 + o % 2
-
-            @pl.when(to != s)
-            def _():
-                remote(send4.at[l, o], recv4.at[l, s], send_sem.at[l, 1], recv_sem.at[l, 1], (1, to, t)).start()
-
-        loop(0, OWNERS, go4)
+        for part in range(2):
+            for d in range(OWNERS):
+                o = lax.rem(jnp.where(owns, owner + 1, s) + d, OWNERS)
+                both = jnp.dot(scaled, wgu[l, o, :, 256 * part:256 * (part + 1)], preferred_element_type=F32).astype(BF)
+                send4[l, part, o] = both
+                send = remote(send4.at[l, part, o], recv4.at[l, part, s], send_sem.at[l, 1 + part],
+                              recv_sem.at[l, 1 + part], (1, 4 * (o // 2) + 1 + o % 2, t))
+                if d < OWNERS - 1:
+                    send.start()
+                else:
+                    pl.when(jnp.logical_not(owns))(send.start)
+
+                    @pl.when(owns)
+                    def _():
+                        recv4[l, part, s] = both
+
+            if part == 0:
+                loop(1, SHARDS, lambda d: send_squares(l, d))
+
+        pl.when(l == 0)(turn_keys)
         factor = squares_factor(l)
         column = jnp.sum(jnp.where(diagonal, factor, 0.0), axis=1, keepdims=True)
 
         @pl.when(owns)
         def _():
-            wait_bytes(recv4.at[l, pl.ds(0, SHARDS - 1)], recv_sem.at[l, 1])
-            both = jnp.sum(recv4[l].astype(F32), axis=0) * column
-            gate, up = both[:, :256], both[:, 256:]
-            hidden = (gate / (1.0 + jnp.exp(-gate)) * up).astype(BF)
-            send5[l] = hidden
-            recv5[l, owner] = hidden
-            loop(1, SHARDS, lambda d: remote(
-                send5.at[l], recv5.at[l, owner], send_sem.at[l, 2], recv_sem.at[l, 2],
-                (1, shard_peer(d), t)).start())
+            for part in range(2):
+                wait_bytes(recv4.at[l, part, pl.ds(0, SHARDS - 1)], recv_sem.at[l, 1 + part])
+                both = jnp.sum(recv4[l, part].astype(F32), axis=0) * column
+                gate, up = both[:, :HD], both[:, HD:]
+                hidden = (gate / (1.0 + jnp.exp(-gate)) * up).astype(BF)
+                send5[l, part] = hidden
+                recv5[l, owner, part] = hidden
+                loop(1, SHARDS, lambda d: remote(
+                    send5.at[l, part], recv5.at[l, owner, part], send_sem.at[l, 3], recv_sem.at[l, 3],
+                    (1, shard_peer(d), t)).start())
 
         @pl.when(l == 0)
         def _():
@@ -351,13 +362,13 @@
 
         @pl.when(owns)
         def _():
-            wait_bytes(recv5.at[l, pl.ds(0, OWNERS - 1)], recv_sem.at[l, 2])
+            wait_bytes(recv5.at[l, pl.ds(0, OWNERS - 1)], recv_sem.at[l, 3])
 
         @pl.when(jnp.logical_not(owns))
         def _():
-            wait_bytes(recv5.at[l], recv_sem.at[l, 2])
-
-        hidden_all = jnp.concatenate([recv5[l, o] for o in range(OWNERS)], axis=1)
+            wait_bytes(recv5.at[l], recv_sem.at[l, 3])
+
+        hidden_all = jnp.concatenate([recv5[l, o, part] for o in range(OWNERS) for part in range(2)], axis=1)
         partial = jnp.dot(hidden_all, wdn[l], preferred_element_type=F32).astype(BF)
         send6[l] = partial
 
@@ -365,7 +376,7 @@
         def _():
             recv6[t] = partial
             loop(1, TPS, lambda d: remote(
-                send6.at[l], recv6.at[t], send_sem.at[l, 3], recv6_sem, (1, s, tp_peer(d))).start())
+                send6.at[l], recv6.at[t], send_sem.at[l, 4], recv6_sem, (1, s, tp_peer(d))).start())
             wait_bytes(recv6.at[pl.ds(0, TPS - 1)], recv6_sem)
             result = (a_buf[...].astype(F32) + jnp.sum(recv6[...].astype(F32), axis=0)).astype(BF)
             x_buf[...] = result
@@ -374,14 +385,13 @@
         @pl.when(l == 1)
         def _():
             loop(0, TPS, lambda d: remote(
-                send6.at[l], recv6.at[t], send_sem.at[l, 3], recv6_sem, (0, s, tp_peer(d))).start())
+                send6.at[l], recv6.at[t], send_sem.at[l, 4], recv6_sem, (0, s, tp_peer(d))).start())
 
     @pl.when(side == 1)
     def _():
         prepare(0)
         for load in first_loads:
             load.wait()
-        turn_keys()
         pl.semaphore_wait(barrier, SHARDS - 1 + TPS - 1 + TPS)
 
     def step(l):
@@ -418,18 +428,22 @@
             wait_bytes(ss_recv.at[l, pl.ds(0, SHARDS - 1)], ss_send_sem.at[l])
             wait_bytes(recv3.at[l, pl.ds(0, TPS - 1)], send_sem.at[l, 0])
 
+            for part in range(2):
+                @pl.when(owns)
+                def _():
+                    wait_bytes(recv4.at[l, part, pl.ds(0, OWNERS - 1)], send_sem.at[l, 1 + part])
+
+                @pl.when(jnp.logical_not(owns))
+                def _():
+                    wait_bytes(recv4.at[l, part, pl.ds(0, OWNERS)], send_sem.at[l, 1 + part])
+
             @pl.when(owns)
             def _():
-                wait_bytes(recv4.at[l, pl.ds(0, OWNERS - 1)], send_sem.at[l, 1])
-                wait_bytes(recv4.at[l, pl.ds(0, SHARDS - 1), :, pl.ds(0, 256)], send_sem.at[l, 2])
-
-            @pl.when(jnp.logical_not(owns))
-            def _():
-                wait_bytes(recv4.at[l, pl.ds(0, OWNERS)], send_sem.at[l, 1])
+                wait_bytes(recv4.at[l, 0, pl.ds(0, SHARDS - 1)], send_sem.at[l, 3])
 
         loop(0, 2, sent)
-        wait_bytes(recv6.at[pl.ds(0, TPS - 1)], send_sem.at[0, 3])
-        wait_bytes(recv6, send_sem.at[1, 3])
+        wait_bytes(recv6.at[pl.ds(0, TPS - 1)], send_sem.at[0, 4])
+        wait_bytes(recv6, send_sem.at[1, 4])
         wait_bytes(a_buf, end_send.at[0])
         wait_bytes(end_scale, end_send.at[1])
 
@@ -455,14 +469,14 @@
             pltpu.VMEM((ROWS, 256), BF), pltpu.VMEM((ROWS, 256), BF),
             pltpu.VMEM((3, 1, HD), F32), pltpu.VMEM((3, SHARDS, 1, HD), F32),
             pltpu.VMEM((16 * SHARDS, HD), F32), pltpu.VMEM((SHARDS, 16, HD), BF), pltpu.VMEM((SHARDS, 16, HD), BF),
-            pltpu.VMEM((16, HD), BF), pltpu.VMEM((2, SHARDS, 16, HD), BF), pltpu.VMEM((16 * SHARDS, HD), F32),
+            pltpu.VMEM((8, HD), BF), pltpu.VMEM((2, SHARDS, 8, HD), BF), pltpu.VMEM((8 * SHARDS, HD), F32),
             pltpu.VMEM((2, ROWS, 256), BF), pltpu.VMEM((2, TPS, ROWS, 256), BF),
-            pltpu.VMEM((2, OWNERS, ROWS, 512), BF), pltpu.VMEM((2, SHARDS, ROWS, 512), BF),
-            pltpu.VMEM((2, ROWS, 256), BF), pltpu.VMEM((2, OWNERS, ROWS, 256), BF),
+            pltpu.VMEM((2, 2, OWNERS, ROWS, 256), BF), pltpu.VMEM((2, 2, SHARDS, ROWS, 256), BF),
+            pltpu.VMEM((2, 2, ROWS, HD), BF), pltpu.VMEM((2, OWNERS, 2, ROWS, HD), BF),
             pltpu.VMEM((2, ROWS, 256), BF), pltpu.VMEM((TPS, ROWS, 256), BF),
             pltpu.VMEM((1, HD), F32),
             dma((12,)), dma((TILES,)), dma((3,)), dma((3,)), dma, dma, dma, dma((2,)),
-            dma((2, 4)), dma((2, 3)), dma, dma((4,)), dma((4,)), dma((2,)), dma((2,)),
+            dma((2, 5)), dma((2, 4)), dma, dma((4,)), dma((4,)), dma((2,)), dma((2,)),
         ],
         compiler_params=pltpu.CompilerParams(
             collective_id=0, has_side_effects=True, vmem_limit_bytes=63 * 1024 * 1024),

time: 73.5 us -> 71.8 us (0.977)
  Pallas kernels: 71.5 us -> 69.8 us
    pallas_call x1, Pallas kernels: 71.5 us -> 69.8 us  [body(): pl.pallas_call(kernel, out_shape=(pltpu.VMEM((ROWS, 256), BF), pltpu.VMEM...]
where the time goes in v5:
time: 71.8 us; the launch traced here: 71.6 us
  Pallas kernels  69.8 us (97%)
  local copies, waits for them, and re-layouts  1.17 us (2%)
    pallas_call x1, Pallas kernels, body(): pl.pallas_call(kernel, out_shape=(pltpu.VMEM((ROWS, 256), BF), pltpu.VMEM...  69.8 us

profile of v5, /device:TPU:6, one launch (start us, length us, event | category | flops | bytes accessed | tf_op | source)
XLA Modules:
  0.0 71.6 jit_solution(13159232496736877518)
XLA Ops:
  0.6 69.8 %shard_map.113 = (bf16[32,256]{1,0:T(8,128)(2,1)S(1)}, f32[2,32]{1,0:T(2,128)S(1)}) custom-call(bf16[32,256]{1,0:T(8,128)(2,1)} %tok_hbm.1, s32[32]{0:T(128)} %lens_hbm.1, f32[1,256]{1,0:T(1,128)} %again_hbm.1, f32[1,256]{1,0:T(1,128)} %fgain_hbm.1, f32[1,128]{1,0:T(1,128)} %constant.2.clone.freq_hbm, bf16[2,4096,256]{2,1,0:T(8,128)(2,1)} %bitcast.9, ...), custom_call_target="tpu_custom_call" | custom-call | flops 130000000 | bytes 7500000 | tf_op jit(solution)/shard_map/pallas_call | solution.py:457
  70.5 0.6 copy.14
  71.1 0.6 copy.15

commit v6 on v5

--- a/solution.py
+++ b/solution.py
@@ -78,7 +78,7 @@
 
     @pl.when(side == 1)
     def _():
-        loop(0, SHARDS, lambda d: greet((0, shard_peer(d), t)))
+        greet(mate)
         loop(1, SHARDS, lambda d: greet((1, shard_peer(d), t)))
         loop(1, TPS, lambda d: greet((1, s, tp_peer(d))))
 
@@ -180,7 +180,7 @@
 
         @pl.when(side == 0)
         def _():
-            pl.semaphore_wait(barrier, 2 * SHARDS - 1)
+            pl.semaphore_wait(barrier, SHARDS)
 
         def go1(d):
             to = shard_peer(d)

time: 71.8 us -> 71.8 us (level)
  no operation moved by 1% of the time
where the time goes in v6:
time: 71.8 us; the launch traced here: 71.6 us
  Pallas kernels  69.8 us (97%)
  local copies, waits for them, and re-layouts  1.17 us (2%)
    pallas_call x1, Pallas kernels, body(): pl.pallas_call(kernel, out_shape=(pltpu.VMEM((ROWS, 256), BF), pltpu.VMEM...  69.8 us

profile of v6, /device:TPU:6, one launch (start us, length us, event | category | flops | bytes accessed | tf_op | source)
XLA Modules:
  0.0 71.6 jit_solution(3310318518713449606)
XLA Ops:
  0.6 69.8 %shard_map.113 = (bf16[32,256]{1,0:T(8,128)(2,1)S(1)}, f32[2,32]{1,0:T(2,128)S(1)}) custom-call(bf16[32,256]{1,0:T(8,128)(2,1)} %tok_hbm.1, s32[32]{0:T(128)} %lens_hbm.1, f32[1,256]{1,0:T(1,128)} %again_hbm.1, f32[1,256]{1,0:T(1,128)} %fgain_hbm.1, f32[1,128]{1,0:T(1,128)} %constant.2.clone.freq_hbm, bf16[2,4096,256]{2,1,0:T(8,128)(2,1)} %bitcast.9, ...), custom_call_target="tpu_custom_call" | custom-call | flops 130000000 | bytes 7500000 | tf_op jit(solution)/shard_map/pallas_call | solution.py:457
  70.5 0.6 copy.14
  71.1 0.6 copy.15

commit v7 on v6

--- a/solution.py
+++ b/solution.py
@@ -167,7 +167,6 @@
             first_loads[2].wait()
 
         values = x_buf[...].astype(F32)
-        put_squares(values, 2)
         mixed = jnp.dot((values * again[...]).astype(BF), wqkv[...], preferred_element_type=F32)
         for part in range(6):
             stage[pl.ds(part, ROWS, stride=8), :] = mixed[:, HD * part:HD * (part + 1)]
@@ -187,6 +186,7 @@
             remote(send1.at[to], recv1.at[s], send1_sem, recv1_sem, (side, to, t)).start()
 
         loop(1, SHARDS, go1)
+        put_squares(values, 2)
         loop(1, SHARDS, lambda d: send_squares(2, d))
 
         @pl.when(side == 0)
@@ -309,7 +309,6 @@
         after = (x_buf[...].astype(F32) + jnp.sum(recv3[l].astype(F32), axis=0)).astype(BF)
         a_buf[...] = after
         values = after.astype(F32)
-        put_squares(values, l)
         scaled = (values * fgain[l]).astype(BF)
 
         for part in range(2):
@@ -329,6 +328,7 @@
                         recv4[l, part, s] = both
 
             if part == 0:
+                put_squares(values, l)
                 loop(1, SHARDS, lambda d: send_squares(l, d))
 
         pl.when(l == 0)(turn_keys)

time: 71.8 us -> 71.8 us (level)
  no operation moved by 1% of the time
where the time goes in v7:
time: 71.8 us; the launch traced here: 71.7 us
  Pallas kernels  69.8 us (97%)
  local copies, waits for them, and re-layouts  1.17 us (2%)
    pallas_call x1, Pallas kernels, body(): pl.pallas_call(kernel, out_shape=(pltpu.VMEM((ROWS, 256), BF), pltpu.VMEM...  69.8 us

profile of v7, /device:TPU:6, one launch (start us, length us, event | category | flops | bytes accessed | tf_op | source)
XLA Modules:
  0.0 71.7 jit_solution(15295735578437154037)
XLA Ops:
  0.6 69.8 %shard_map.113 = (bf16[32,256]{1,0:T(8,128)(2,1)S(1)}, f32[2,32]{1,0:T(2,128)S(1)}) custom-call(bf16[32,256]{1,0:T(8,128)(2,1)} %tok_hbm.1, s32[32]{0:T(128)} %lens_hbm.1, f32[1,256]{1,0:T(1,128)} %again_hbm.1, f32[1,256]{1,0:T(1,128)} %fgain_hbm.1, f32[1,128]{1,0:T(1,128)} %constant.2.clone.freq_hbm, bf16[2,4096,256]{2,1,0:T(8,128)(2,1)} %bitcast.9, ...), custom_call_target="tpu_custom_call" | custom-call | flops 130000000 | bytes 7500000 | tf_op jit(solution)/shard_map/pallas_call | solution.py:457
  70.5 0.6 copy.14
  71.1 0.6 copy.15
